TPU v7x, 512 devices: a whole 4x8x8 slice. The times are simulated.
512 devices in a mesh: cap: 4 (over z_lo), clip: 32 (over z_hi, y, core), frame: 4 (over x).
Axes of the slice: x: 4, y: 8, z: 8 (z_hi: 2, z_lo: 4; z = z_hi * 4 + z_lo), core: 2. Of those that a mesh axis runs over, the one named last changes fastest.
Arguments:
- cap_tokens: float32 [32, 32, 512], P('cap', 'clip')
- clip_tokens: float32 [32, 16, 50, 512], P('clip', 'frame')
- win_frame: int32 [32, 32, 32], P('cap', None, 'clip'), may hold values from 0 to 15
- win_patch: int32 [32, 32, 32], P('cap', None, 'clip'), may hold values from 0 to 49
- cap_lengths: int32 [32], P('cap'), may hold values from 8 to 32
Outputs:
- loss: float32 [], replicated
- cap_grad: float32 [32, 32, 512], P('cap', 'clip')
- clip_grad: float32 [32, 16, 50, 512], P('clip', 'frame', None, 'cap')
All inputs are finite; a program needn't handle non-finite values.
Results may differ from a plain program's by a relative error of at most 0.00009.
Values sent between devices are 32-bit elements; how exact they have to be, the bound alone decides.
A program may use at most 64 MiB of HBM per device.

v0:
```python
import jax
import jax.numpy as jnp
from jax import lax
from jax.sharding import PartitionSpec as P

logit_scale = 1.0 / 0.07
norm_eps = 1e-06
highest = lax.Precision.HIGHEST


def unit_rows(values):
    inverse = lax.rsqrt(jnp.sum(values * values, axis=-1, keepdims=True) + norm_eps)
    return (values * inverse, inverse)


def body(cap_tokens, clip_tokens, win_frame, win_patch, cap_lengths):
    cap_count = lax.axis_size("cap")
    cap_block, tok_local, emb_width = cap_tokens.shape
    clip_block, frame_local, patches, _ = clip_tokens.shape
    tok_all = win_frame.shape[1]
    columns = frame_local * patches
    key_count = clip_block * columns
    query_count = cap_block * tok_all
    cap_unit, cap_inverse = unit_rows(cap_tokens)
    clip_unit, clip_inverse = unit_rows(clip_tokens)
    key_rows = clip_unit.reshape(key_count, emb_width)
    clip_scale = clip_inverse.reshape(key_count, 1)
    gathered = lax.all_gather(cap_unit, "clip", axis=1, tiled=True)
    queries = gathered.reshape(query_count, emb_width)
    local_frame = win_frame - lax.axis_index("frame") * frame_local
    present = (local_frame >= 0) & (local_frame < frame_local)
    clip_offset = lax.broadcasted_iota(jnp.int32, (1, 1, clip_block), 2) * columns
    row_index = jnp.where(present, clip_offset + local_frame * patches + win_patch, 0)
    flat_index = row_index.reshape(query_count, clip_block)
    present_f = present.astype(jnp.float32)
    dense = jnp.einsum("qe,re->qr", queries, key_rows, precision=highest)
    picked = (
        jnp.take_along_axis(dense, flat_index, axis=1).reshape(cap_block, tok_all, clip_block)
        * present_f
    )
    live_mask = (
        lax.broadcasted_iota(jnp.int32, (cap_block, tok_all), 1) < cap_lengths[:, None]
    ).astype(jnp.float32)
    length_f = cap_lengths.astype(jnp.float32)
    partial_score = jnp.sum(live_mask[:, :, None] * picked, axis=1) / length_f[:, None]
    scores = lax.psum(partial_score, "frame")
    logits = logit_scale * scores
    exp_logits = jnp.exp(logits)
    cap_ids = lax.axis_index("cap") * cap_block + lax.broadcasted_iota(jnp.int32, (cap_block, 1), 0)
    clip_ids = lax.axis_index("clip") * clip_block + lax.broadcasted_iota(
        jnp.int32, (1, clip_block), 1
    )
    positive = (cap_ids == clip_ids).astype(jnp.float32)
    row_total = lax.psum(jnp.sum(exp_logits, axis=1), "clip")
    col_total = lax.psum(jnp.sum(exp_logits, axis=0), "cap")
    local_loss = jnp.where(lax.axis_index("clip") == 0, jnp.sum(jnp.log(row_total)), 0.0)
    local_loss = local_loss + jnp.where(
        lax.axis_index("cap") == 0, jnp.sum(jnp.log(col_total)), 0.0
    )
    local_loss = local_loss - 2.0 * jnp.sum(positive * logits)
    total = 0.5 * lax.psum(local_loss, ("cap", "clip"))
    loss = total / (cap_count * cap_block)
    logit_grad = (
        0.5 * (exp_logits / row_total[:, None] + exp_logits / col_total[None, :]) - positive
    )
    score_grad = logit_scale * logit_grad
    token_weight = score_grad[:, None, :] * (live_mask / length_f[:, None])[:, :, None] * present_f
    query_ids = lax.broadcasted_iota(jnp.int32, (query_count, clip_block), 0)
    weight_table = (
        jnp.zeros((query_count, key_count), jnp.float32)
        .at[query_ids, flat_index]
        .add(token_weight.reshape(query_count, clip_block))
    )
    shaped_table = weight_table.reshape(cap_block, tok_all, key_count)
    part_grad = lax.psum_scatter(
        jnp.einsum("ctr,re->tce", shaped_table, key_rows, precision=highest),
        "clip",
        scatter_dimension=0,
        tiled=True,
    )
    own_grad = jnp.transpose(lax.psum(part_grad, "frame"), (1, 0, 2))
    cap_inner = jnp.sum(cap_unit * own_grad, axis=-1, keepdims=True)
    cap_grad = cap_inverse * (own_grad - cap_unit * cap_inner)
    clip_unit_grad = jnp.einsum("qr,qe->re", weight_table, queries, precision=highest)
    share_width = emb_width // cap_count
    share_begin = lax.axis_index("cap") * share_width
    summed_clip = lax.psum(clip_unit_grad, "cap")
    clip_inner = jnp.sum(key_rows * summed_clip, axis=-1, keepdims=True)
    full_grad = clip_scale * (summed_clip - key_rows * clip_inner)
    clip_share = lax.dynamic_slice_in_dim(full_grad, share_begin, share_width, 1)
    clip_grad = clip_share.reshape(clip_block, frame_local, patches, share_width)
    return (loss, cap_grad, clip_grad)


def solution(mesh):
    placed = (
        P("cap", "clip", None),
        P("clip", "frame", None, None),
        P("cap", None, "clip"),
        P("cap", None, "clip"),
        P("cap"),
    )
    return jax.shard_map(
        body,
        mesh=mesh,
        in_specs=placed,
        out_specs=(P(), P("cap", "clip", None), P("clip", "frame", None, "cap")),
        check_vma=False,
    )
```

profile of v0, /device:TPU:256, one launch (start us, length us, event | category | flops | bytes accessed | tf_op | source)
XLA Modules:
  0.0 555.8 jit_solution(15174552686839854831)
XLA Ops:
  8.0 0.0 copy-start
  8.0 0.0 all-reduce.2.cloned.1.call-start
  8.1 1.2 multiply_reduce_fusion.1
  9.3 0.0 copy-done
  9.3 0.1 broadcast_multiply_fusion
  9.4 0.1 copy.33
  9.6 0.0 copy-start.1
  9.6 0.1 reshape.278
  9.6 0.7 copy-done.1
  10.3 0.1 multiply_reduce_fusion.3
  10.4 0.1 copy_multiply_fusion
  10.5 49.7 %all_gather.3 = f32[8,32,512]{2,0,1:T(8,128)S(1)} all-gather(f32[8,1,512]{2,0,1:T(8,128)S(1)} %copy_multiply_fusion), channel_id=1, replica_groups=mesh['cap'=4,'clip'=32,'frame'=4] {'clip'}, dimensions={1}, use_global_device_ids=true | all-gather | bytes 540672 | tf_op jit(solution)/shard_map/all_gather | solution.py:28
  60.3 0.0 copy-start.3
  60.3 0.3 copy.30
  60.6 0.0 copy-start.2
  60.6 0.5 broadcast.269
  61.1 0.0 copy-done.3
  61.1 0.2 copy-done.2
  61.3 0.7 fusion.15
  61.9 0.1 reshape.279
  62.1 0.7 fusion.16
  62.7 2.4 gather_fusion
  65.1 0.1 gather.7
  65.2 0.0 copy-start.4
  65.2 0.7 copy-done.4
  65.9 0.2 fusion.6
  66.1 10.5 %psum.42 = f32[8,1]{0,1:T(1,128)S(1)} all-reduce(f32[8,1]{0,1:T(1,128)S(1)} %divide_bitcast_fusion), channel_id=1, replica_groups=mesh['cap'=4,'clip'=32,'frame'=4] {'frame'}, use_global_device_ids=true, to_apply=%region_3.4 | all-reduce | flops 8 | bytes 64 | tf_op jit(solution)/shard_map/psum | solution.py:46
  76.6 0.6 fusion.8
  77.2 12.6 %psum.44 = f32[1]{0:T(128)} all-reduce(f32[1]{0:T(128)} %bitcast.5), channel_id=1, replica_groups=mesh['cap'=4,'clip'=32,'frame'=4] {'cap'}, use_global_device_ids=true, to_apply=%region_7.8 | all-reduce | flops 1 | bytes 8 | tf_op jit(solution)/shard_map/psum | solution.py:55
  89.7 84.2 %psum.43 = f32[8]{0:T(128)S(1)} all-reduce(f32[8]{0:T(128)S(1)} %get-tuple-element.21), channel_id=1, replica_groups=mesh['cap'=4,'clip'=32,'frame'=4] {'clip'}, use_global_device_ids=true, to_apply=%region_4.5 | all-reduce | flops 8 | bytes 64 | tf_op jit(solution)/shard_map/psum | solution.py:54
  174.0 0.7 fusion.11
  174.6 0.1 fusion.4
  174.7 0.1 reshape.295
  174.8 13.0 %scatter_fusion = f32[256,200]{0,1:T(8,128)S(1)} fusion(f32[256,200]{0,1:T(8,128)S(1)} %broadcast_in_dim.11, s32[256]{0:T(256)S(1)} %bitcast.31, f32[256]{0:T(256)S(1)} %reshape.295), kind=kCustom, calls=%fused_computation.1 | custom fusion | flops 256 | bytes 5120 | tf_op jit(solution)/shard_map/scatter-add | solution.py:72
  187.9 1.3 fusion.17
  189.2 0.0 all-reduce.2.cloned.1.call-update
  189.2 0.0 reduce-scatter.2.cloned.1.call-start
  189.3 0.1 copy.34
  189.4 0.1 reshape.301
  189.4 0.6 convolution_bitcast_fusion
  190.1 1.1 copy.35
  191.2 0.0 reduce-scatter.2.cloned.1.call-update
  191.9 0.6 log_reduce_fusion
  193.8 334.1 %psum.45 = f32[]{:T(128)} all-reduce(f32[]{:T(128)S(6)} %sub.20), channel_id=1, replica_groups=mesh['cap'=4,'clip'=32,'frame'=4] {'cap','clip'}, use_global_device_ids=true, to_apply=%region_9.10 | all-reduce | flops 1 | bytes 8 | tf_op jit(solution)/shard_map/psum | solution.py:61
  527.9 0.1 copy.38
  528.0 0.1 rsqrt.25
  528.7 0.0 all-reduce.2.cloned.1.call-done
  528.7 1.1 multiply_reduce_fusion
  529.9 1.0 fusion
  530.9 0.7 copy.37
  531.6 0.0 reduce-scatter.2.cloned.1.call-done
  531.6 14.8 %psum.46 = f32[8,1,512]{2,0,1:T(8,128)S(1)} all-reduce(f32[8,1,512]{2,0,1:T(8,128)} %bitcast.36), channel_id=1, replica_groups=mesh['cap'=4,'clip'=32,'frame'=4] {'frame'}, use_global_device_ids=true, to_apply=%region_12.13 | all-reduce | flops 4096 | bytes 32768 | tf_op jit(solution)/shard_map/psum | solution.py:81
  546.4 0.2 multiply_reduce_fusion.2
  546.6 0.1 subtract_multiply_fusion
  546.6 0.6 copy.36
  (10 shorter events, 0.1 us)
Async XLA Ops:
  8.0 1.3 copy-start
  8.0 520.7 %all-reduce.2.cloned.1.call-start = ((), (), s32[]{:S(2)}) async-start(), calls=%async_computation.2 | async-start | bytes 819200 | tf_op jit(solution)/shard_map/psum | solution.py:87
  9.6 0.7 copy-start.1
  60.3 0.8 copy-start.3
  60.6 0.7 copy-start.2
  65.2 0.7 copy-start.4
  189.2 342.4 %reduce-scatter.2.cloned.1.call-start = ((), (), s32[]{:S(2)}) async-start(), calls=%async_computation.1 | async-start | bytes 540672 | tf_op jit(solution)/shard_map/reduce_scatter | solution.py:75
Sparse Core Ops, SparseCore 0:
  189.3 49.5 all-reduce.1
Sparse Core Ops, SparseCore 1:
  194.2 116.6 reduce-scatter.1
where the time goes:
time: 556 us
  blocking collectives  506 us (91%)
  other arithmetic  19.9 us (4%)
  between operations  19.5 us (4%)
  local copies, waits for them, and re-layouts  7.86 us (1%)
    psum x1, blocking collectives, body(): total = 0.5 * lax.psum(local_loss, ('cap', 'clip'))  334 us
    psum x1, blocking collectives, body(): row_total = lax.psum(jnp.sum(exp_logits, axis=1), 'clip')  84.2 us
    all_gather x1, blocking collectives, body(): gathered = lax.all_gather(cap_unit, 'clip', axis=1, tiled=True)  49.7 us
    psum x1, blocking collectives, body(): own_grad = jnp.transpose(lax.psum(part_grad, 'frame'), (1, 0, 2))  14.8 us
    scatter-add x1, other arithmetic, body(): weight_table = jnp.zeros((query_count, key_count), jnp.float32).at[query_...  13 us
    psum x1, blocking collectives, body(): col_total = lax.psum(jnp.sum(exp_logits, axis=0), 'cap')  12.6 us
  transfers between devices with their start and end apart: 2, of which 0 were waited for; matrix products, arithmetic and copies ran while one was open for 1% of the time, Pallas kernels for 0%

commit v1 on v0

v1 whole, which is shorter than its diff:
```python
import functools

import jax
import jax.numpy as jnp
from jax import lax
from jax.experimental import pallas as pl
from jax.experimental.pallas import tpu as pltpu
from jax.sharding import PartitionSpec as P

MESH = pl.DeviceIdType.MESH
logit_scale = 1.0 / 0.07
norm_eps = 1e-06
f32 = jnp.float32
bf16 = jnp.bfloat16
LANES = 128
SUB = 8


def iota(shape, dim):
    return lax.broadcasted_iota(jnp.int32, shape, dim)


def two_terms(x):
    high = x.astype(bf16)
    return high, (x - high.astype(f32)).astype(bf16)


def three_terms(x):
    high = x.astype(bf16).astype(f32)
    rest = x - high
    middle = rest.astype(bf16).astype(f32)
    return high, middle, rest - middle


def dot(a, b):
    return jnp.dot(a, b, preferred_element_type=f32)


def times_exact(tile, table):
    high, middle, low = three_terms(tile)
    stacked = jnp.concatenate([high, middle, low, jnp.zeros_like(high)], axis=0).astype(bf16)
    out = dot(stacked, table)
    return out[0:SUB] + out[SUB : 2 * SUB] + out[2 * SUB : 3 * SUB]


def kernel(
    nc, nv, patches,
    cap_ref, clip_ref, wf_ref, wp_ref, len_ref,
    loss_ref, cap_out, clip_out,
    cap_raw, clip_raw, wf_raw, wp_raw, qn, give, trade, q_full, keys, key_inv, key_cat, column, picked_rows,
    rows_in, tiles_in, logits_in, tile_out, grads_in, grad_out, one_hot, cap_res, clip_res,
    load_sem, store_sem, trade_send, trade_recv, key_send, key_recv, gather_send, gather_recv, spread_send,
    spread_recv, rows_send, rows_recv, tile_send, tile_recv, logit_send, logit_recv, grad_send, grad_recv,
):
    nf = nc
    tok = nv
    me_c, me_v, me_f = lax.axis_index("cap"), lax.axis_index("clip"), lax.axis_index("frame")
    rows = 4 * patches
    all_rows = nf * rows
    per_block = tok * SUB
    all_tokens = nf * per_block

    loads = [
        pltpu.make_async_copy(clip_ref, clip_raw, load_sem.at[0]),
        pltpu.make_async_copy(cap_ref, cap_raw, load_sem.at[1]),
        pltpu.make_async_copy(wf_ref, wf_raw, load_sem.at[2]),
        pltpu.make_async_copy(wp_ref, wp_raw, load_sem.at[3]),
    ]
    for load in loads:
        load.start()

    barrier = pltpu.get_barrier_semaphore()

    def device(dc, dv, df):
        return {
            "cap": lax.rem(me_c + dc, nc),
            "clip": lax.rem(me_v + dv, nv),
            "frame": lax.rem(me_f + df, nf),
        }

    def signal(dc, dv, df):
        pl.semaphore_signal(barrier, inc=1, device_id=device(dc, dv, df), device_id_type=MESH)

    @pl.loop(1, nc * nf)
    def _(step):
        signal(step // nf, 0, lax.rem(step, nf))

    @pl.loop(1, nv)
    def _(step):
        signal(0, step, 0)

    lane = iota((SUB, LANES), 1)
    sub = iota((SUB, LANES), 0)
    group = lane // tok
    slot_in_group = lax.rem(lane, tok)

    loads[1].wait()
    raw = [cap_raw[pl.ds(j, SUB, stride=nc), :] for j in range(nc)]
    total = raw[0] * raw[0]
    for j in range(1, nc):
        total = total + raw[j] * raw[j]
    cap_inv = lax.rsqrt(jnp.sum(total, axis=1, keepdims=True) + norm_eps)
    loads[2].wait()
    loads[3].wait()
    lengths = jnp.zeros((SUB, LANES), f32)
    for c in range(SUB):
        lengths = jnp.where(sub == c, len_ref[c].astype(f32), lengths)
    frame_own = wf_raw[...].astype(f32)
    patch_own = wp_raw[...].astype(f32)
    give[:, 2 * SUB : 3 * SUB, :] = jnp.zeros((nc, SUB, LANES), f32)
    give[:, SUB : 2 * SUB, :] = jnp.zeros((nc, SUB, LANES), f32)
    for j in range(nc):
        unit = raw[j] * cap_inv
        qn[j] = unit
        give[j, 0:SUB, :] = unit
        give[j, SUB : 2 * SUB, 0:tok] = frame_own
        give[j, 2 * SUB : 3 * SUB, 0:tok] = patch_own
        give[j, 3 * SUB : 4 * SUB, :] = lengths

    loads[0].wait()
    whole = clip_raw[...].reshape(patches, nc // 2, SUB, LANES)
    square = whole * whole
    summed = square[:, 0]
    for j in range(1, nc // 2):
        summed = summed + square[:, j]
    summed = summed + pltpu.roll(summed, 4, 1)
    inverse = lax.rsqrt(jnp.sum(summed, axis=2, keepdims=True) + norm_eps)
    half = clip_raw[:, pl.ds(pl.multiple_of((me_c // 2) * SUB, SUB), SUB), :]
    unit = (half * inverse).reshape(patches // 2, 2, SUB, LANES)
    first, second = unit[:, 0], unit[:, 1]
    low_half = iota((patches // 2, SUB, LANES), 1) < 4
    odd = lax.rem(me_c, 2) == 1
    even_slice = jnp.where(low_half, first, pltpu.roll(second, 4, 1))
    odd_slice = jnp.where(low_half, pltpu.roll(first, 4, 1), second)
    keys[pl.ds(pl.multiple_of(me_f * rows, SUB), rows), :] = jnp.where(odd, odd_slice, even_slice).reshape(rows, LANES)
    inverse = jnp.broadcast_to(inverse, (patches, SUB, LANES)).reshape(patches // 2, 2, SUB, LANES)
    key_inv[...] = jnp.where(low_half, inverse[:, 0], inverse[:, 1]).reshape(rows, LANES)

    pl.semaphore_wait(barrier, nc * nf - 1 + nv - 1)

    def trade_copy(d):
        to = lax.rem(me_c + d, nc)
        return pltpu.make_async_remote_copy(
            src_ref=give.at[to], dst_ref=trade.at[me_c], send_sem=trade_send.at[d], recv_sem=trade_recv.at[d],
            device_id=device(d, 0, 0), device_id_type=MESH,
        )

    def key_copy(d):
        mine = keys.at[pl.ds(pl.multiple_of(me_f * rows, SUB), rows)]
        return pltpu.make_async_remote_copy(
            src_ref=mine, dst_ref=mine, send_sem=key_send.at[d], recv_sem=key_recv.at[d],
            device_id=device(0, 0, d), device_id_type=MESH,
        )

    trades = [trade_copy(d) for d in range(1, nc)]
    key_copies = [key_copy(d) for d in range(1, nf)]
    for copy in trades:
        copy.start()
    for copy in key_copies:
        copy.start()
    trade[me_c] = give[me_c]
    for copy in trades:
        copy.wait()

    own_rows = pl.ds(pl.multiple_of(me_v * SUB, SUB), SUB)
    q_full[me_f, own_rows, :] = trade[me_f, 0:SUB, :]

    def gather_copy(step):
        return pltpu.make_async_remote_copy(
            src_ref=trade.at[me_f, pl.ds(0, SUB)], dst_ref=q_full.at[me_f, own_rows],
            send_sem=gather_send, recv_sem=gather_recv, device_id=device(0, step, 0), device_id_type=MESH,
        )

    @pl.loop(1, nv)
    def _(step):
        gather_copy(step).start()

    def row_number(frame, patch):
        return (frame // 4) * rows + patch * 4 + lax.rem(frame, 4)

    winner = row_number(
        trade[me_f, SUB : 2 * SUB, :].astype(jnp.int32), trade[me_f, 2 * SUB : 3 * SUB, :].astype(jnp.int32)
    )
    for t in range(tok):
        column[t * SUB : (t + 1) * SUB, :] = jnp.broadcast_to(winner[:, t : t + 1], (SUB, LANES))
    wide_lane = iota((per_block, LANES), 1)
    column_value = column[...]
    padded = key_cat.shape[0]
    chosen = jnp.concatenate(
        [(column_value == wide_lane + k * LANES).astype(f32).astype(bf16) for k in range(padded // LANES)], axis=1
    )

    frames = jnp.zeros((SUB, LANES), f32)
    patch_all = jnp.zeros((SUB, LANES), f32)
    length = jnp.zeros((SUB, LANES), f32)
    for j in range(nc):
        here = group == j
        frames = jnp.where(here, pltpu.roll(trade[j, SUB : 2 * SUB, :], j * tok, 1), frames)
        patch_all = jnp.where(here, pltpu.roll(trade[j, 2 * SUB : 3 * SUB, :], j * tok, 1), patch_all)
        length = jnp.where(here, trade[j, 3 * SUB : 4 * SUB, :], length)
    frames = frames.astype(jnp.int32)
    live = (slot_in_group.astype(f32) < length) & (group < nc)
    safe_length = jnp.maximum(length, 1.0)
    local = jnp.where(
        (frames // 4 == me_f) & (group < nc), patch_all.astype(jnp.int32) * 4 + lax.rem(frames, 4), 255
    )
    from_lane = iota((LANES, all_tokens), 0)
    token = iota((LANES, all_tokens), 1)
    spread = (
        (from_lane == (token // per_block) * tok + lax.rem(token, per_block) // SUB).astype(f32).astype(bf16)
    )
    mine_of = lax.rem(iota((SUB, all_tokens), 1), SUB) == iota((SUB, all_tokens), 0)

    def as_row(values):
        return jnp.sum(jnp.where(mine_of, values, 0.0), axis=0, keepdims=True)

    twice = jnp.concatenate([local.astype(f32), jnp.zeros((SUB, LANES), f32)], axis=0).astype(bf16)
    local_row = as_row(dot(twice, spread)[0:SUB]).astype(jnp.int32)
    hit = (iota((rows, all_tokens), 0) == local_row).astype(f32)
    one_hot[...] = hit.astype(bf16)
    same_group = ((iota((LANES, LANES), 0) // tok) == (iota((LANES, LANES), 1) // tok)).astype(f32).astype(bf16)

    for copy in key_copies:
        copy.wait()
    if padded > all_rows:
        key_cat[all_rows:padded, :] = jnp.zeros((padded - all_rows, 2 * LANES), bf16)
    high, low = two_terms(keys[...])
    key_cat[0:all_rows, 0:LANES] = high
    key_cat[0:all_rows, LANES:] = low
    both = dot(chosen, key_cat[...])
    picked = both[:, 0:LANES] + both[:, LANES:]
    picked_rows[...] = picked

    gathered = pltpu.make_async_copy(
        q_full.at[0, pl.ds(0, (nv - 1) * SUB)], q_full.at[0, pl.ds(0, (nv - 1) * SUB)], gather_recv
    )
    gathered.wait()
    product = picked * q_full[me_f]
    tile = jnp.zeros((SUB, LANES), f32)
    for t in range(tok):
        value = jnp.sum(product[t * SUB : (t + 1) * SUB, :], axis=1, keepdims=True)
        tile = jnp.where(lane == me_f * tok + t, value, tile)
    tile_out[0] = tile

    me_16 = me_c * nf + me_f
    tiles_in[me_16] = tile

    def tile_copy(step):
        return pltpu.make_async_remote_copy(
            src_ref=tile_out.at[0], dst_ref=tiles_in.at[me_16], send_sem=tile_send, recv_sem=tile_recv,
            device_id=device(step // nf, 0, lax.rem(step, nf)), device_id_type=MESH,
        )

    @pl.loop(1, nc * nf)
    def _(step):
        tile_copy(step).start()

    rows_in[me_v] = picked_rows[own_rows, :]

    def rows_copy(step):
        to = lax.rem(me_v + step, nv)
        return pltpu.make_async_remote_copy(
            src_ref=picked_rows.at[pl.ds(pl.multiple_of(to * SUB, SUB), SUB)], dst_ref=rows_in.at[me_v],
            send_sem=rows_send, recv_sem=rows_recv, device_id=device(0, step, 0), device_id_type=MESH,
        )

    @pl.loop(1, nv)
    def _(step):
        rows_copy(step).start()

    def spread_copy(d):
        return pltpu.make_async_remote_copy(
            src_ref=q_full.at[me_f], dst_ref=q_full.at[me_f], send_sem=spread_send.at[d], recv_sem=spread_recv.at[d],
            device_id=device(0, 0, d), device_id_type=MESH,
        )

    spreads = [spread_copy(d) for d in range(1, nf)]
    for copy in spreads:
        copy.start()

    pltpu.make_async_copy(
        tiles_in.at[pl.ds(0, nc * nf - 1)], tiles_in.at[pl.ds(0, nc * nf - 1)], tile_recv
    ).wait()
    all_picked = jnp.sum(tiles_in[...], axis=0)
    live_share = jnp.where(live, all_picked, 0.0)
    scores = times_exact(live_share, same_group) / safe_length
    own_logits = logit_scale * scores
    logit_tile = jnp.where((slot_in_group == me_v) & (group < nc), own_logits, 0.0)
    tile_out[1] = logit_tile
    logits_in[me_v] = logit_tile

    def logit_copy(step):
        return pltpu.make_async_remote_copy(
            src_ref=tile_out.at[1], dst_ref=logits_in.at[me_v], send_sem=logit_send, recv_sem=logit_recv,
            device_id=device(0, step, 0), device_id_type=MESH,
        )

    @pl.loop(1, nv)
    def _(step):
        logit_copy(step).start()

    share_row = as_row(times_exact(live_share / safe_length, spread))
    caption_of = iota((all_tokens, LANES), 0)
    caption_lane = (caption_of // per_block) * (LANES // nc) + lax.rem(caption_of, SUB)
    by_caption = (iota((all_tokens, LANES), 1) == caption_lane).astype(f32).astype(bf16)
    share_high, share_low = two_terms(hit * share_row)
    inner_table = dot(share_high, by_caption) + dot(share_low, by_caption)

    pltpu.make_async_copy(logits_in.at[pl.ds(0, nv - 1)], logits_in.at[pl.ds(0, nv - 1)], logit_recv).wait()
    logits = jnp.sum(logits_in[...], axis=0)
    used = group < nc
    exp_logits = jnp.where(used, jnp.exp(logits), 0.0)
    row_total = times_exact(exp_logits, same_group)
    col = jnp.broadcast_to(jnp.sum(exp_logits, axis=0, keepdims=True), (SUB, LANES))
    col_total = col
    for j in range(1, LANES // tok):
        col_total = col_total + pltpu.roll(col, j * tok, 1)
    positive = jnp.where(used & (slot_in_group == group * SUB + sub), 1.0, 0.0)
    grad = logit_scale * (0.5 * (exp_logits / row_total + exp_logits / col_total) - positive)
    weight = jnp.where(used, grad / safe_length, 0.0)

    block_weight = jnp.zeros((SUB, LANES), f32)
    block_length = jnp.zeros((SUB, LANES), f32)
    for j in range(nc):
        here = me_f == j
        shifted = pltpu.roll(weight, (LANES - j * tok) % LANES, 1)
        block_weight = jnp.where(here, shifted, block_weight)
        block_length = jnp.where(here, trade[j, 3 * SUB : 4 * SUB, :], block_length)
    slice_grad = jnp.zeros((SUB, LANES), f32)
    for v in range(nv):
        slice_grad = slice_grad + block_weight[:, v : v + 1] * rows_in_value(rows_in, rows_recv, nv, v)
    slice_grad = jnp.where(me_v.astype(f32) < block_length, slice_grad, 0.0)
    grad_out[...] = slice_grad
    self_last = me_c == me_f

    def grad_copy(df):
        return pltpu.make_async_remote_copy(
            src_ref=grad_out, dst_ref=grads_in.at[me_c], send_sem=grad_send.at[df], recv_sem=grad_recv.at[me_c],
            device_id={"cap": me_f, "clip": me_v, "frame": df}, device_id_type=MESH,
        )

    for df in range(nf):
        to_self = self_last & (me_f == df)

        @pl.when(jnp.logical_not(to_self))
        def _():
            grad_copy(df).start()

        @pl.when(to_self)
        def _():
            grads_in[me_c] = slice_grad

    own = jnp.where(slot_in_group == me_v, grad, 0.0)
    row_weight = jnp.zeros((SUB, LANES), f32)
    token_weight = []
    for j in range(nc):
        value = jnp.sum(jnp.where(group == j, own, 0.0), axis=1, keepdims=True)
        row_weight = jnp.where(lane == j * (LANES // nc) + sub, value, row_weight)
        token_weight.append(value / jnp.maximum(trade[j, 3 * SUB : 4 * SUB, :], 1.0))
    inner = jnp.sum(inner_table * jnp.sum(row_weight, axis=0, keepdims=True), axis=1, keepdims=True)
    for copy in spreads:
        copy.wait()
    when = iota((tok, SUB, LANES), 0).astype(f32)
    parts = []
    for j in range(nc):
        mask = when < trade[j, 3 * SUB : 4 * SUB, :][None]
        scaled = q_full[j].reshape(tok, SUB, LANES) * jnp.where(mask, token_weight[j][None], 0.0)
        parts.append(jnp.concatenate(two_terms(scaled.reshape(per_block, LANES)), axis=1))
    both = dot(one_hot[...], jnp.concatenate(parts, axis=0))
    own_keys = keys[pl.ds(pl.multiple_of(me_f * rows, SUB), rows), :]
    clip_res[...] = key_inv[...] * (both[:, 0:LANES] + both[:, LANES:] - own_keys * inner)
    clip_store = pltpu.make_async_copy(clip_res, clip_out, store_sem.at[0])
    clip_store.start()

    terms = jnp.where((slot_in_group == 0) & used, jnp.log(row_total), 0.0)
    terms = terms + jnp.where((lane < tok) & (sub == 0), jnp.log(col_total), 0.0)
    terms = 0.5 * terms - positive * logits
    loss_ref[0, 0] = jnp.sum(terms) / (nc * SUB)

    for j in range(nc):

        @pl.when(jnp.logical_not(self_last & (me_c == j)))
        def _():
            pltpu.make_async_copy(grad_out, grads_in.at[j], grad_recv.at[j]).wait()

    dot_tile = jnp.zeros((SUB, LANES), f32)
    for j in range(nc):
        dot_tile = dot_tile + qn[j] * grads_in[j]
    cap_inner = jnp.sum(dot_tile, axis=1, keepdims=True)
    for j in range(nc):
        cap_res[pl.ds(j, SUB, stride=nc), :] = cap_inv * (grads_in[j] - qn[j] * cap_inner)
    cap_store = pltpu.make_async_copy(cap_res, cap_out, store_sem.at[1])
    cap_store.start()

    pltpu.make_async_copy(
        q_full.at[0, pl.ds(0, (nv - 1) * SUB)], q_full.at[0, pl.ds(0, (nv - 1) * SUB)], gather_send
    ).wait()
    pltpu.make_async_copy(rows_in.at[pl.ds(0, nv - 1)], rows_in.at[pl.ds(0, nv - 1)], rows_send).wait()
    pltpu.make_async_copy(logits_in.at[pl.ds(0, nv - 1)], logits_in.at[pl.ds(0, nv - 1)], logit_send).wait()
    pltpu.make_async_copy(
        tiles_in.at[pl.ds(0, nc * nf - 1)], tiles_in.at[pl.ds(0, nc * nf - 1)], tile_send
    ).wait()
    for df in range(nf):

        @pl.when(jnp.logical_not(self_last & (me_f == df)))
        def _():
            pltpu.make_async_copy(grad_out, grads_in.at[0], grad_send.at[df]).wait()

    clip_store.wait()
    cap_store.wait()


def rows_in_value(rows_in, rows_recv, nv, v):
    if v == 0:
        pltpu.make_async_copy(rows_in.at[pl.ds(0, nv - 1)], rows_in.at[pl.ds(0, nv - 1)], rows_recv).wait()
    return rows_in[v]


def body(nc, nv, cap_tokens, clip_tokens, win_frame, win_patch, cap_lengths):
    block, _, width = cap_tokens.shape
    _, frames, patches, _ = clip_tokens.shape
    assert block == SUB and frames == 4 and width == nc * LANES and win_frame.shape == (SUB, nv, 1)
    rows = frames * patches
    per_block = nv * SUB
    padded = -(-nc * rows // LANES) * LANES
    caps = cap_tokens.reshape(SUB * nc, LANES)
    clips = clip_tokens.reshape(frames, patches, nc, LANES).transpose(1, 2, 0, 3).reshape(patches, nc * frames, LANES)
    vmem = pltpu.VMEM
    dma = pltpu.SemaphoreType.DMA
    scratch = [
        vmem((SUB * nc, LANES), f32),
        vmem((patches, nc * frames, LANES), f32),
        vmem((SUB, nv), jnp.int32),
        vmem((SUB, nv), jnp.int32),
        vmem((nc, SUB, LANES), f32),
        vmem((nc, 4 * SUB, LANES), f32),
        vmem((nc, 4 * SUB, LANES), f32),
        vmem((nc, per_block, LANES), f32),
        vmem((nc * rows, LANES), f32),
        vmem((rows, LANES), f32),
        vmem((padded, 2 * LANES), bf16),
        vmem((per_block, LANES), jnp.int32),
        vmem((per_block, LANES), f32),
        vmem((nv, SUB, LANES), f32),
        vmem((nc * nc, SUB, LANES), f32),
        vmem((nv, SUB, LANES), f32),
        vmem((2, SUB, LANES), f32),
        vmem((nc, SUB, LANES), f32),
        vmem((SUB, LANES), f32),
        vmem((rows, nc * per_block), bf16),
        vmem((SUB * nc, LANES), f32),
        vmem((rows, LANES), f32),
        dma((4,)), dma((2,)),
        dma((nc,)), dma((nc,)), dma((nc,)), dma((nc,)),
        dma, dma,
        dma((nc,)), dma((nc,)),
        dma, dma, dma, dma, dma, dma,
        dma((nc,)), dma((nc,)),
    ]
    hbm = pl.BlockSpec(memory_space=pl.ANY)
    smem = pl.BlockSpec(memory_space=pltpu.SMEM)
    loss, cap_grad, clip_grad = pl.pallas_call(
        functools.partial(kernel, nc, nv, patches),
        out_shape=(
            jax.ShapeDtypeStruct((1, 1), f32),
            jax.ShapeDtypeStruct((SUB * nc, LANES), f32),
            jax.ShapeDtypeStruct((rows, LANES), f32),
        ),
        in_specs=[hbm, hbm, hbm, hbm, smem],
        out_specs=(smem, hbm, hbm),
        scratch_shapes=scratch,
        compiler_params=pltpu.CompilerParams(
            collective_id=0, has_side_effects=True, vmem_limit_bytes=32 * 1024 * 1024
        ),
    )(caps, clips, win_frame.reshape(SUB, nv), win_patch.reshape(SUB, nv), cap_lengths)
    clip_grad = clip_grad.reshape(patches, frames, LANES).transpose(1, 0, 2)[None]
    return loss.reshape(()), cap_grad.reshape(SUB, 1, width), clip_grad


def solution(mesh):
    placed = (
        P("cap", "clip", None),
        P("clip", "frame", None, None),
        P("cap", None, "clip"),
        P("cap", None, "clip"),
        P("cap"),
    )
    assert mesh.shape["cap"] == mesh.shape["frame"]
    return jax.shard_map(
        functools.partial(body, mesh.shape["cap"], mesh.shape["clip"]),
        mesh=mesh,
        in_specs=placed,
        out_specs=(P(), P("cap", "clip", None), P("clip", "frame", None, "cap")),
        check_vma=False,
    )
```

time: 556 us -> 58.8 us (0.11)
  the two profiles are of different devices: /device:TPU:256 before, /device:TPU:1 now
where the time goes in v1:
time: 58.8 us; the launch traced here: 58.6 us
  Pallas kernels  51.9 us (88%)
  local copies, waits for them, and re-layouts  4.33 us (7%)
  between operations  2.35 us (4%)
    pallas_call x1, Pallas kernels, body(): pl.pallas_call(functools.partial(kernel, nc, nv, patches), out_shape=(jax...  51.9 us
    unnamed x12, local copies, waits for them, and re-layouts  4.33 us

profile of v1, /device:TPU:1, one launch (start us, length us, event | category | flops | bytes accessed | tf_op | source)
XLA Modules:
  0.0 58.6 jit_solution(9068901591525335640)
XLA Ops:
  0.6 0.0 copy-start.2
  0.6 0.0 copy-start.4
  0.7 0.7 %copy-done.2 = s32[8,32,1]{1,2,0:T(1,128)S(1)} copy-done((s32[8,32,1]{1,2,0:T(1,128)S(1)}, s32[8,32,1]{1,2,0:T(1,128)}, u32[]{:S(2)}) %copy-start.2) | copy-done | bytes 1048
  1.3 0.0 copy-done.4
  1.3 0.0 copy-start
  1.3 1.0 %copy-done = f32[1,4,50,512]{3,1,2,0:T(4,128)S(1)} copy-done((f32[1,4,50,512]{3,1,2,0:T(4,128)S(1)}, f32[1,4,50,512]{3,1,2,0:T(4,128)}, u32[]{:S(2)}) %copy-start) | copy-done | bytes 409624
  2.3 0.0 copy-start.1
  2.3 0.7 %copy-done.1 = f32[8,1,512]{2,1,0:T(1,128)S(1)} copy-done((f32[8,1,512]{2,1,0:T(1,128)S(1)}, f32[8,1,512]{2,1,0:T(1,128)}, u32[]{:S(2)}) %copy-start.1) | copy-done | bytes 16408
  3.0 0.0 copy-start.3
  3.0 0.7 %copy-done.3 = s32[8,32,1]{1,2,0:T(1,128)S(1)} copy-done((s32[8,32,1]{1,2,0:T(1,128)S(1)}, s32[8,32,1]{1,2,0:T(1,128)}, u32[]{:S(2)}) %copy-start.3) | copy-done | bytes 1048
  3.7 51.9 %shard_map.76 = (f32[1,1]{1,0:T(1,128)}, f32[32,128]{1,0:T(8,128)S(1)}, f32[200,128]{1,0:T(8,128)S(1)}) custom-call(f32[32,128]{1,0:T(8,128)S(1)} %bitcast.18, f32[50,16,128]{2,1,0:T(8,128)S(1)} %bitcast.15, s32[8,32]{1,0:T(8,128)S(1)} %bitcast.19, s32[8,32]{1,0:T(8,128)S(1)} %bitcast.20, s32[8]{0:T(128)S(1)} %copy-done.4), custom_call_target="tpu_custom_call" | custom-call | tf_op jit(solution)/shard_map/pallas_call | solution.py:462
  56.2 0.6 %copy.14 = f32[8,1,512]{2,1,0:T(1,128)} copy(f32[8,1,512]{2,1,0:T(1,128)S(1)} %bitcast.17) | data formatting | bytes 32768
  56.8 0.6 %copy.15 = f32[1,4,50,128]{3,1,2,0:T(4,128)} copy(f32[1,4,50,128]{3,1,2,0:T(4,128)S(1)} %bitcast.16) | data formatting | bytes 204800
Async XLA Ops:
  0.6 0.7 %copy-start.2 = (s32[8,32,1]{1,2,0:T(1,128)S(1)}, s32[8,32,1]{1,2,0:T(1,128)}, u32[]{:S(2)}) copy-start(s32[8,32,1]{1,2,0:T(1,128)} %param.7) | copy-start | bytes 3076
  0.6 0.7 %copy-start.4 = (s32[8]{0:T(128)S(1)}, s32[8]{0:T(128)}, u32[]{:S(2)}) copy-start(s32[8]{0:T(128)} %len_ref.1) | copy-start | bytes 100
  1.3 1.0 %copy-start = (f32[1,4,50,512]{3,1,2,0:T(4,128)S(1)}, f32[1,4,50,512]{3,1,2,0:T(4,128)}, u32[]{:S(2)}) copy-start(f32[1,4,50,512]{3,1,2,0:T(4,128)} %param.6) | copy-start | bytes 1228804
  2.3 0.7 %copy-start.1 = (f32[8,1,512]{2,1,0:T(1,128)S(1)}, f32[8,1,512]{2,1,0:T(1,128)}, u32[]{:S(2)}) copy-start(f32[8,1,512]{2,1,0:T(1,128)} %param.5) | copy-start | bytes 49156
  3.0 0.7 %copy-start.3 = (s32[8,32,1]{1,2,0:T(1,128)S(1)}, s32[8,32,1]{1,2,0:T(1,128)}, u32[]{:S(2)}) copy-start(s32[8,32,1]{1,2,0:T(1,128)} %param.8) | copy-start | bytes 3076

commit v2 on v1

v2 whole, which is shorter than its diff:
```python
import functools

import jax
import jax.numpy as jnp
from jax import lax
from jax.experimental import pallas as pl
from jax.experimental.pallas import tpu as pltpu
from jax.sharding import PartitionSpec as P

MESH = pl.DeviceIdType.MESH
logit_scale = 1.0 / 0.07
norm_eps = 1e-06
f32 = jnp.float32
bf16 = jnp.bfloat16
LANES = 128
SUB = 8


def iota(shape, dim):
    return lax.broadcasted_iota(jnp.int32, shape, dim)


def two_terms(x):
    high = x.astype(bf16)
    return high, (x - high.astype(f32)).astype(bf16)


def three_terms(x):
    high = x.astype(bf16).astype(f32)
    rest = x - high
    middle = rest.astype(bf16).astype(f32)
    return high, middle, rest - middle


def dot(a, b):
    return jnp.dot(a, b, preferred_element_type=f32)


def times_exact(tile, table):
    high, middle, low = three_terms(tile)
    stacked = jnp.concatenate([high, middle, low, jnp.zeros_like(high)], axis=0).astype(bf16)
    out = dot(stacked, table)
    return out[0:SUB] + out[SUB : 2 * SUB] + out[2 * SUB : 3 * SUB]


def log2(n):
    assert n & (n - 1) == 0
    return n.bit_length() - 1


def kernel(
    nc, nv, patches,
    cap_ref, clip_ref, wf_ref, wp_ref, len_ref,
    loss_ref, cap_out, clip_out,
    cap_raw, clip_raw, wf_raw, wp_raw, qn, give, trade, q_full, q_pick, unit_keys, keys, key_inv, key_cat, column,
    picked_rows, rows_in, tiles_in, logits_in, tile_out, grads_in, grad_out, spread_table, caption_table, one_hot,
    cap_res, clip_res,
    load_sem, store_sem, trade_send, trade_recv, key_send, key_recv, pick_send, pick_recv, gather_send, gather_recv,
    spread_send, spread_recv, rows_send, rows_recv, tile_send, tile_recv, logit_send, logit_recv, grad_send, grad_recv,
):
    nf = nc
    tok = nv
    me_c, me_v, me_f = lax.axis_index("cap"), lax.axis_index("clip"), lax.axis_index("frame")
    rows = 4 * patches
    all_rows = nf * rows
    per_block = tok * SUB
    all_tokens = nf * per_block
    tok_bits, block_bits = log2(tok), log2(per_block)

    loads = [
        pltpu.make_async_copy(clip_ref, clip_raw, load_sem.at[0]),
        pltpu.make_async_copy(cap_ref, cap_raw, load_sem.at[1]),
        pltpu.make_async_copy(wf_ref, wf_raw, load_sem.at[2]),
        pltpu.make_async_copy(wp_ref, wp_raw, load_sem.at[3]),
    ]
    for load in loads:
        load.start()

    barrier = pltpu.get_barrier_semaphore()

    def device(dc, dv, df):
        return {
            "cap": lax.rem(me_c + dc, nc),
            "clip": lax.rem(me_v + dv, nv),
            "frame": lax.rem(me_f + df, nf),
        }

    def signal(dc, dv, df):
        pl.semaphore_signal(barrier, inc=1, device_id=device(dc, dv, df), device_id_type=MESH)

    @pl.loop(1, nc * nf)
    def _(step):
        signal(step // nf, 0, lax.rem(step, nf))

    @pl.loop(1, nv)
    def _(step):
        signal(0, step, 0)

    lane = iota((SUB, LANES), 1)
    sub = iota((SUB, LANES), 0)
    group = lane >> tok_bits
    slot_in_group = lane & (tok - 1)
    used = group < nc

    loads[1].wait()
    raw = [cap_raw[pl.ds(j, SUB, stride=nc), :] for j in range(nc)]
    total = raw[0] * raw[0]
    for j in range(1, nc):
        total = total + raw[j] * raw[j]
    cap_inv = lax.rsqrt(jnp.sum(total, axis=1, keepdims=True) + norm_eps)
    for j in range(nc):
        unit = raw[j] * cap_inv
        qn[j] = unit
        give[j, 0:SUB, :] = unit

    loads[0].wait()
    whole = clip_raw[...].reshape(patches, nc // 2, SUB, LANES)
    square = whole * whole
    summed = square[:, 0]
    for j in range(1, nc // 2):
        summed = summed + square[:, j]
    summed = summed + pltpu.roll(summed, 4, 1)
    inverse = lax.rsqrt(jnp.sum(summed, axis=2, keepdims=True) + norm_eps)
    low_half = iota((patches // 2, SUB, LANES), 1) < 4
    for j in range(nc // 2):
        unit = (whole[:, j] * inverse).reshape(patches // 2, 2, SUB, LANES)
        first, second = unit[:, 0], unit[:, 1]
        unit_keys[2 * j] = jnp.where(low_half, first, pltpu.roll(second, 4, 1)).reshape(rows, LANES)
        unit_keys[2 * j + 1] = jnp.where(low_half, pltpu.roll(first, 4, 1), second).reshape(rows, LANES)
    inverse = jnp.broadcast_to(inverse, (patches, SUB, LANES)).reshape(patches // 2, 2, SUB, LANES)
    key_inv[...] = jnp.where(low_half, inverse[:, 0], inverse[:, 1]).reshape(rows, LANES)

    pl.semaphore_wait(barrier, nc * nf - 1 + nv - 1)

    own_key_rows = pl.ds(pl.multiple_of(me_f * rows, SUB), rows)
    own_rows = pl.ds(pl.multiple_of(me_v * SUB, SUB), SUB)

    def key_copy(d):
        return pltpu.make_async_remote_copy(
            src_ref=unit_keys.at[lax.rem(me_f + d, nf)], dst_ref=keys.at[own_key_rows],
            send_sem=key_send.at[d], recv_sem=key_recv.at[d], device_id=device(0, 0, d), device_id_type=MESH,
        )

    key_copies = [key_copy(d) for d in range(1, nf)]
    for copy in key_copies:
        copy.start()

    @pl.loop(1, nv)
    def _(step):
        pltpu.make_async_remote_copy(
            src_ref=qn.at[me_f], dst_ref=q_pick.at[own_rows],
            send_sem=pick_send, recv_sem=pick_recv, device_id=device(0, step, 0), device_id_type=MESH,
        ).start()

    loads[2].wait()
    loads[3].wait()
    lengths = jnp.zeros((SUB, LANES), f32)
    for c in range(SUB):
        lengths = jnp.where(sub == c, len_ref[c].astype(f32), lengths)
    give[:, SUB : 3 * SUB, :] = jnp.zeros((nc, 2 * SUB, LANES), f32)
    for j in range(nc):
        give[j, SUB : 2 * SUB, 0:tok] = wf_raw[...].astype(f32)
        give[j, 2 * SUB : 3 * SUB, 0:tok] = wp_raw[...].astype(f32)
        give[j, 3 * SUB : 4 * SUB, :] = lengths

    def trade_copy(d):
        to = lax.rem(me_c + d, nc)
        return pltpu.make_async_remote_copy(
            src_ref=give.at[to], dst_ref=trade.at[me_c], send_sem=trade_send.at[d], recv_sem=trade_recv.at[d],
            device_id=device(d, 0, 0), device_id_type=MESH,
        )

    trades = [trade_copy(d) for d in range(1, nc)]
    for copy in trades:
        copy.start()
    trade[me_c] = give[me_c]
    keys[own_key_rows, :] = unit_keys[me_f]
    q_pick[own_rows, :] = qn[me_f]

    frame_own = wf_raw[...]
    winner = (frame_own >> 2) * rows + wp_raw[...] * 4 + (frame_own & 3)
    for t in range(tok):
        column[t * SUB : (t + 1) * SUB, :] = jnp.broadcast_to(winner[:, t : t + 1], (SUB, LANES))
    wide_lane = iota((per_block, LANES), 1)
    column_value = column[...]
    padded = key_cat.shape[0]
    chosen = jnp.concatenate(
        [(column_value == wide_lane + k * LANES).astype(f32).astype(bf16) for k in range(padded // LANES)], axis=1
    )
    if padded > all_rows:
        key_cat[all_rows:padded, :] = jnp.zeros((padded - all_rows, 2 * LANES), bf16)

    from_lane = iota((LANES, all_tokens), 0)
    token = iota((LANES, all_tokens), 1)
    spread_table[...] = (
        (from_lane == ((token >> block_bits) << tok_bits) + ((token & (per_block - 1)) >> 3)).astype(f32).astype(bf16)
    )
    caption_of = iota((all_tokens, LANES), 0)
    caption_lane = (caption_of >> block_bits) * (LANES // nc) + (caption_of & 7)
    caption_table[...] = (iota((all_tokens, LANES), 1) == caption_lane).astype(f32).astype(bf16)
    same_group = ((iota((LANES, LANES), 0) >> tok_bits) == (iota((LANES, LANES), 1) >> tok_bits)).astype(f32).astype(bf16)
    mine_of = (iota((SUB, all_tokens), 1) & 7) == iota((SUB, all_tokens), 0)

    def as_row(values):
        return jnp.sum(jnp.where(mine_of, values, 0.0), axis=0, keepdims=True)

    for copy in trades:
        copy.wait()
    q_full[me_f, own_rows, :] = trade[me_f, 0:SUB, :]

    @pl.loop(1, nv)
    def _(step):
        pltpu.make_async_remote_copy(
            src_ref=trade.at[me_f, pl.ds(0, SUB)], dst_ref=q_full.at[me_f, own_rows],
            send_sem=gather_send, recv_sem=gather_recv, device_id=device(0, step, 0), device_id_type=MESH,
        ).start()

    frames = jnp.zeros((SUB, LANES), f32)
    patch_all = jnp.zeros((SUB, LANES), f32)
    length = jnp.zeros((SUB, LANES), f32)
    for j in range(nc):
        here = group == j
        frames = jnp.where(here, pltpu.roll(trade[j, SUB : 2 * SUB, :], j * tok, 1), frames)
        patch_all = jnp.where(here, pltpu.roll(trade[j, 2 * SUB : 3 * SUB, :], j * tok, 1), patch_all)
        length = jnp.where(here, trade[j, 3 * SUB : 4 * SUB, :], length)
    frames = frames.astype(jnp.int32)
    live = (slot_in_group.astype(f32) < length) & used
    safe_length = jnp.maximum(length, 1.0)
    local = jnp.where(((frames >> 2) == me_f) & used, patch_all.astype(jnp.int32) * 4 + (frames & 3), 255)
    twice = jnp.concatenate([local.astype(f32), jnp.zeros((SUB, LANES), f32)], axis=0).astype(bf16)
    local_row = as_row(dot(twice, spread_table[...])[0:SUB]).astype(jnp.int32)
    one_hot[...] = (iota((rows, all_tokens), 0) == local_row).astype(f32).astype(bf16)

    for copy in key_copies:
        copy.wait()
    high, low = two_terms(keys[...])
    key_cat[0:all_rows, 0:LANES] = high
    key_cat[0:all_rows, LANES:] = low
    both = dot(chosen, key_cat[...])
    picked = both[:, 0:LANES] + both[:, LANES:]
    picked_rows[...] = picked

    all_but_one = pl.ds(0, (nv - 1) * SUB)
    pltpu.make_async_copy(q_pick.at[all_but_one], q_pick.at[all_but_one], pick_recv).wait()
    product = picked * q_pick[...]
    tile = jnp.zeros((SUB, LANES), f32)
    for t in range(tok):
        value = jnp.sum(product[t * SUB : (t + 1) * SUB, :], axis=1, keepdims=True)
        tile = jnp.where(lane == me_c * tok + t, value, tile)
    tile_out[0] = tile

    me_16 = me_c * nf + me_f
    tiles_in[me_16] = tile

    @pl.loop(1, nc * nf)
    def _(step):
        pltpu.make_async_remote_copy(
            src_ref=tile_out.at[0], dst_ref=tiles_in.at[me_16], send_sem=tile_send, recv_sem=tile_recv,
            device_id=device(step // nf, 0, lax.rem(step, nf)), device_id_type=MESH,
        ).start()

    rows_in[me_v] = picked_rows[own_rows, :]

    @pl.loop(1, nv)
    def _(step):
        to = lax.rem(me_v + step, nv)
        pltpu.make_async_remote_copy(
            src_ref=picked_rows.at[pl.ds(pl.multiple_of(to * SUB, SUB), SUB)], dst_ref=rows_in.at[me_v],
            send_sem=rows_send, recv_sem=rows_recv, device_id=device(0, step, 0), device_id_type=MESH,
        ).start()

    other_tiles = tiles_in.at[pl.ds(0, nc * nf - 1)]
    other_clips = rows_in.at[pl.ds(0, nv - 1)]
    pltpu.make_async_copy(other_tiles, other_tiles, tile_recv).wait()
    all_picked = jnp.sum(tiles_in[...], axis=0)
    live_share = jnp.where(live, all_picked, 0.0)
    own_logits = logit_scale * (times_exact(live_share, same_group) / safe_length)
    logit_tile = jnp.where((slot_in_group == me_v) & used, own_logits, 0.0)
    tile_out[1] = logit_tile
    logits_in[me_v] = logit_tile

    @pl.loop(1, nv)
    def _(step):
        pltpu.make_async_remote_copy(
            src_ref=tile_out.at[1], dst_ref=logits_in.at[me_v], send_sem=logit_send, recv_sem=logit_recv,
            device_id=device(0, step, 0), device_id_type=MESH,
        ).start()

    gathered = q_full.at[0, all_but_one]
    pltpu.make_async_copy(gathered, gathered, gather_recv).wait()

    def spread_copy(d):
        return pltpu.make_async_remote_copy(
            src_ref=q_full.at[me_f], dst_ref=q_full.at[me_f], send_sem=spread_send.at[d], recv_sem=spread_recv.at[d],
            device_id=device(0, 0, d), device_id_type=MESH,
        )

    spreads = [spread_copy(d) for d in range(1, nf)]
    for copy in spreads:
        copy.start()

    share_row = as_row(times_exact(live_share / safe_length, spread_table[...]))
    share_high, share_low = two_terms(one_hot[...].astype(f32) * share_row)
    inner_table = dot(share_high, caption_table[...]) + dot(share_low, caption_table[...])
    pltpu.make_async_copy(other_clips, other_clips, rows_recv).wait()

    pltpu.make_async_copy(other_clips, other_clips, logit_recv).wait()
    logits = jnp.sum(logits_in[...], axis=0)
    exp_logits = jnp.where(used, jnp.exp(logits), 0.0)
    row_total = times_exact(exp_logits, same_group)
    col = jnp.broadcast_to(jnp.sum(exp_logits, axis=0, keepdims=True), (SUB, LANES))
    col_total = col
    for j in range(1, LANES // tok):
        col_total = col_total + pltpu.roll(col, j * tok, 1)
    positive = jnp.where(used & (slot_in_group == group * SUB + sub), 1.0, 0.0)
    grad = logit_scale * (0.5 * (exp_logits / row_total + exp_logits / col_total) - positive)
    weight = jnp.where(used, grad / safe_length, 0.0)

    block_weight = jnp.zeros((SUB, LANES), f32)
    for j in range(nc):
        block_weight = jnp.where(me_c == j, pltpu.roll(weight, (LANES - j * tok) % LANES, 1), block_weight)
    slice_grad = jnp.zeros((SUB, LANES), f32)
    for v in range(nv):
        slice_grad = slice_grad + block_weight[:, v : v + 1] * rows_in[v]
    slice_grad = jnp.where(me_v.astype(f32) < lengths, slice_grad, 0.0)
    grad_out[...] = slice_grad
    grads_in[me_f] = slice_grad

    def grad_copy(d):
        return pltpu.make_async_remote_copy(
            src_ref=grad_out, dst_ref=grads_in.at[me_f], send_sem=grad_send.at[d], recv_sem=grad_recv.at[d],
            device_id=device(0, 0, d), device_id_type=MESH,
        )

    grad_copies = [grad_copy(d) for d in range(1, nf)]
    for copy in grad_copies:
        copy.start()

    own = jnp.where(slot_in_group == me_v, grad, 0.0)
    row_weight = jnp.zeros((SUB, LANES), f32)
    token_weight = []
    for j in range(nc):
        value = jnp.sum(jnp.where(group == j, own, 0.0), axis=1, keepdims=True)
        row_weight = jnp.where(lane == j * (LANES // nc) + sub, value, row_weight)
        token_weight.append(value / jnp.maximum(trade[j, 3 * SUB : 4 * SUB, :], 1.0))
    inner = jnp.sum(inner_table * jnp.sum(row_weight, axis=0, keepdims=True), axis=1, keepdims=True)
    for copy in spreads:
        copy.wait()
    when = iota((tok, SUB, LANES), 0).astype(f32)
    parts = []
    for j in range(nc):
        mask = when < trade[j, 3 * SUB : 4 * SUB, :][None]
        scaled = q_full[j].reshape(tok, SUB, LANES) * jnp.where(mask, token_weight[j][None], 0.0)
        parts.append(jnp.concatenate(two_terms(scaled.reshape(per_block, LANES)), axis=1))
    both = dot(one_hot[...], jnp.concatenate(parts, axis=0))
    clip_res[...] = key_inv[...] * (both[:, 0:LANES] + both[:, LANES:] - unit_keys[me_c] * inner)
    clip_store = pltpu.make_async_copy(clip_res, clip_out, store_sem.at[0])
    clip_store.start()

    terms = jnp.where((slot_in_group == 0) & used, jnp.log(row_total), 0.0)
    terms = terms + jnp.where((lane < tok) & (sub == 0), jnp.log(col_total), 0.0)
    terms = 0.5 * terms - positive * logits
    loss_ref[0, 0] = jnp.sum(terms) / (nc * SUB)

    for copy in grad_copies:
        copy.wait()
    dot_tile = jnp.zeros((SUB, LANES), f32)
    for j in range(nc):
        dot_tile = dot_tile + qn[j] * grads_in[j]
    cap_inner = jnp.sum(dot_tile, axis=1, keepdims=True)
    for j in range(nc):
        cap_res[pl.ds(j, SUB, stride=nc), :] = cap_inv * (grads_in[j] - qn[j] * cap_inner)
    cap_store = pltpu.make_async_copy(cap_res, cap_out, store_sem.at[1])
    cap_store.start()

    pltpu.make_async_copy(gathered, gathered, pick_send).wait()
    pltpu.make_async_copy(gathered, gathered, gather_send).wait()
    pltpu.make_async_copy(other_clips, other_clips, rows_send).wait()
    pltpu.make_async_copy(other_clips, other_clips, logit_send).wait()
    pltpu.make_async_copy(other_tiles, other_tiles, tile_send).wait()
    clip_store.wait()
    cap_store.wait()


def body(nc, nv, cap_tokens, clip_tokens, win_frame, win_patch, cap_lengths):
    block, _, width = cap_tokens.shape
    _, frames, patches, _ = clip_tokens.shape
    assert block == SUB and frames == 4 and width == nc * LANES and win_frame.shape == (SUB, nv, 1)
    rows = frames * patches
    per_block = nv * SUB
    padded = -(-nc * rows // LANES) * LANES
    caps = cap_tokens.reshape(SUB * nc, LANES)
    clips = clip_tokens.reshape(frames, patches, nc, LANES).transpose(1, 2, 0, 3).reshape(patches, nc * frames, LANES)
    vmem = pltpu.VMEM
    dma = pltpu.SemaphoreType.DMA
    scratch = [
        vmem((SUB * nc, LANES), f32),
        vmem((patches, nc * frames, LANES), f32),
        vmem((SUB, nv), jnp.int32),
        vmem((SUB, nv), jnp.int32),
        vmem((nc, SUB, LANES), f32),
        vmem((nc, 4 * SUB, LANES), f32),
        vmem((nc, 4 * SUB, LANES), f32),
        vmem((nc, per_block, LANES), f32),
        vmem((per_block, LANES), f32),
        vmem((nc, rows, LANES), f32),
        vmem((nc * rows, LANES), f32),
        vmem((rows, LANES), f32),
        vmem((padded, 2 * LANES), bf16),
        vmem((per_block, LANES), jnp.int32),
        vmem((per_block, LANES), f32),
        vmem((nv, SUB, LANES), f32),
        vmem((nc * nc, SUB, LANES), f32),
        vmem((nv, SUB, LANES), f32),
        vmem((2, SUB, LANES), f32),
        vmem((nc, SUB, LANES), f32),
        vmem((SUB, LANES), f32),
        vmem((LANES, nc * per_block), bf16),
        vmem((nc * per_block, LANES), bf16),
        vmem((rows, nc * per_block), bf16),
        vmem((SUB * nc, LANES), f32),
        vmem((rows, LANES), f32),
        dma((4,)), dma((2,)),
        dma((nc,)), dma((nc,)), dma((nc,)), dma((nc,)),
        dma, dma, dma, dma,
        dma((nc,)), dma((nc,)),
        dma, dma, dma, dma, dma, dma,
        dma((nc,)), dma((nc,)),
    ]
    hbm = pl.BlockSpec(memory_space=pl.ANY)
    smem = pl.BlockSpec(memory_space=pltpu.SMEM)
    loss, cap_grad, clip_grad = pl.pallas_call(
        functools.partial(kernel, nc, nv, patches),
        out_shape=(
            jax.ShapeDtypeStruct((1, 1), f32),
            jax.ShapeDtypeStruct((SUB * nc, LANES), f32),
            jax.ShapeDtypeStruct((rows, LANES), f32),
        ),
        in_specs=[hbm, hbm, hbm, hbm, smem],
        out_specs=(smem, hbm, hbm),
        scratch_shapes=scratch,
        compiler_params=pltpu.CompilerParams(
            collective_id=0, has_side_effects=True, vmem_limit_bytes=60 * 1024 * 1024
        ),
    )(caps, clips, win_frame.reshape(SUB, nv), win_patch.reshape(SUB, nv), cap_lengths)
    clip_grad = clip_grad.reshape(patches, frames, LANES).transpose(1, 0, 2)[None]
    return loss.reshape(()), cap_grad.reshape(SUB, 1, width), clip_grad


def solution(mesh):
    placed = (
        P("cap", "clip", None),
        P("clip", "frame", None, None),
        P("cap", None, "clip"),
        P("cap", None, "clip"),
        P("cap"),
    )
    assert mesh.shape["cap"] == mesh.shape["frame"]
    return jax.shard_map(
        functools.partial(body, mesh.shape["cap"], mesh.shape["clip"]),
        mesh=mesh,
        in_specs=placed,
        out_specs=(P(), P("cap", "clip", None), P("clip", "frame", None, "cap")),
        check_vma=False,
    )
```

time: 58.8 us -> 52.8 us (0.90)
  Pallas kernels: 51.9 us -> 47.2 us
  local copies, waits for them, and re-layouts: 4.33 us -> 2.87 us
    pallas_call x1, Pallas kernels: 51.9 us -> 47.2 us  [body(): pl.pallas_call(functools.partial(kernel, nc, nv, patches), out_shape=(jax...]
    unnamed x12 -> x2, local copies, waits for them, and re-layouts: 4.33 us -> 2.87 us
where the time goes in v2:
time: 52.8 us; the launch traced here: 52.5 us
  Pallas kernels  47.2 us (89%)
  local copies, waits for them, and re-layouts  2.87 us (5%)
  between operations  2.45 us (5%)
    pallas_call x1, Pallas kernels, body(): pl.pallas_call(functools.partial(kernel, nc, nv, patches), out_shape=(jax...  47.2 us
    unnamed x2, local copies, waits for them, and re-layouts  2.87 us

profile of v2, /device:TPU:1, one launch (start us, length us, event | category | flops | bytes accessed | tf_op | source)
XLA Modules:
  0.0 52.5 jit_solution(1912575552024409739)
XLA Ops:
  0.6 47.2 %shard_map.76 = (f32[1,1]{1,0:T(1,128)}, f32[32,128]{1,0:T(8,128)}, f32[200,128]{1,0:T(8,128)}) custom-call(f32[32,128]{1,0:T(8,128)} %bitcast.18, f32[50,16,128]{2,1,0:T(8,128)} %bitcast.15, s32[8,32]{1,0:T(8,128)} %bitcast.19, s32[8,32]{1,0:T(8,128)} %bitcast.20, s32[8]{0:T(128)} %len_ref.1), custom_call_target="tpu_custom_call" | custom-call | tf_op jit(solution)/shard_map/pallas_call | solution.py:432
  48.5 1.3 %copy.14 = f32[8,1,512]{2,1,0:T(1,128)} copy(f32[8,1,512]{2,1,0:T(1,128)} %bitcast.17) | data formatting | bytes 32768
  49.9 1.5 %copy.15 = f32[1,4,50,128]{3,1,2,0:T(4,128)} copy(f32[1,4,50,128]{3,1,2,0:T(4,128)} %bitcast.16) | data formatting | bytes 204800

commit v3 on v2

--- a/solution.py
+++ b/solution.py
@@ -43,6 +43,10 @@
     return out[0:SUB] + out[SUB : 2 * SUB] + out[2 * SUB : 3 * SUB]
 
 
+def group_of(lane, size):
+    return lane >> log2(size)
+
+
 def log2(n):
     assert n & (n - 1) == 0
     return n.bit_length() - 1
@@ -51,12 +55,12 @@
 def kernel(
     nc, nv, patches,
     cap_ref, clip_ref, wf_ref, wp_ref, len_ref,
-    loss_ref, cap_out, clip_out,
+    loss_ref, cap_res, clip_res,
     cap_raw, clip_raw, wf_raw, wp_raw, qn, give, trade, q_full, q_pick, unit_keys, keys, key_inv, key_cat, column,
-    picked_rows, rows_in, tiles_in, logits_in, tile_out, grads_in, grad_out, spread_table, caption_table, one_hot,
-    cap_res, clip_res,
-    load_sem, store_sem, trade_send, trade_recv, key_send, key_recv, pick_send, pick_recv, gather_send, gather_recv,
-    spread_send, spread_recv, rows_send, rows_recv, tile_send, tile_recv, logit_send, logit_recv, grad_send, grad_recv,
+    picked_rows, rows_in, tiles_in, scores_in, logits_in, tile_out, line_out, weights, turned, grads_in, grad_out, spread_table, caption_table, one_hot,
+    len_raw,
+    load_sem, trade_send, trade_recv, key_send, key_recv, pick_send, pick_recv, gather_send, gather_recv,
+    spread_send, spread_recv, rows_send, rows_recv, tile_send, tile_recv, score_send, score_recv, logit_send, logit_recv, grad_send, grad_recv,
 ):
     nf = nc
     tok = nv
@@ -72,6 +76,7 @@
         pltpu.make_async_copy(cap_ref, cap_raw, load_sem.at[1]),
         pltpu.make_async_copy(wf_ref, wf_raw, load_sem.at[2]),
         pltpu.make_async_copy(wp_ref, wp_raw, load_sem.at[3]),
+        pltpu.make_async_copy(len_ref, len_raw, load_sem.at[4]),
     ]
     for load in loads:
         load.start()
@@ -101,6 +106,8 @@
     group = lane >> tok_bits
     slot_in_group = lane & (tok - 1)
     used = group < nc
+    cap_lanes = LANES // nc
+    in_line = (lane & (cap_lanes - 1)) < SUB
 
     loads[1].wait()
     raw = [cap_raw[pl.ds(j, SUB, stride=nc), :] for j in range(nc)]
@@ -152,11 +159,11 @@
             send_sem=pick_send, recv_sem=pick_recv, device_id=device(0, step, 0), device_id_type=MESH,
         ).start()
 
-    loads[2].wait()
-    loads[3].wait()
-    lengths = jnp.zeros((SUB, LANES), f32)
-    for c in range(SUB):
-        lengths = jnp.where(sub == c, len_ref[c].astype(f32), lengths)
+    for load in loads[2:]:
+        load.wait()
+    diagonal = iota((SUB, SUB), 0) == iota((SUB, SUB), 1)
+    lengths = jnp.sum(jnp.where(diagonal, len_raw[...].astype(f32), 0.0), axis=1, keepdims=True)
+    lengths = jnp.broadcast_to(lengths, (SUB, LANES))
     give[:, SUB : 3 * SUB, :] = jnp.zeros((nc, 2 * SUB, LANES), f32)
     for j in range(nc):
         give[j, SUB : 2 * SUB, 0:tok] = wf_raw[...].astype(f32)
@@ -242,20 +249,33 @@
 
     all_but_one = pl.ds(0, (nv - 1) * SUB)
     pltpu.make_async_copy(q_pick.at[all_but_one], q_pick.at[all_but_one], pick_recv).wait()
-    product = picked * q_pick[...]
+    product = (picked * q_pick[...]).reshape(tok, SUB, LANES)
+
+    when = iota((tok, SUB, LANES), 0).astype(f32)
+    score = jnp.sum(jnp.sum(jnp.where(when < lengths[None], product, 0.0), axis=0), axis=1, keepdims=True)
+    score = score * logit_scale / lengths
+    me_16 = me_c * nf + me_f
+    own_score = pl.ds(me_16, 1)
+    line_out[0:1, :] = jnp.sum(jnp.where(lane == me_c * cap_lanes + sub, score, 0.0), axis=0, keepdims=True)
+    scores_in[own_score, :] = line_out[0:1, :]
+
+    @pl.loop(1, nc * nf)
+    def _(step):
+        pltpu.make_async_remote_copy(
+            src_ref=line_out.at[0:1], dst_ref=scores_in.at[own_score], send_sem=score_send, recv_sem=score_recv,
+            device_id=device(step // nf, 0, lax.rem(step, nf)), device_id_type=MESH,
+        ).start()
+
     tile = jnp.zeros((SUB, LANES), f32)
     for t in range(tok):
-        value = jnp.sum(product[t * SUB : (t + 1) * SUB, :], axis=1, keepdims=True)
-        tile = jnp.where(lane == me_c * tok + t, value, tile)
-    tile_out[0] = tile
-
-    me_16 = me_c * nf + me_f
+        tile = jnp.where(lane == me_c * tok + t, jnp.sum(product[t], axis=1, keepdims=True), tile)
+    tile_out[...] = tile
     tiles_in[me_16] = tile
 
     @pl.loop(1, nc * nf)
     def _(step):
         pltpu.make_async_remote_copy(
-            src_ref=tile_out.at[0], dst_ref=tiles_in.at[me_16], send_sem=tile_send, recv_sem=tile_recv,
+            src_ref=tile_out, dst_ref=tiles_in.at[me_16], send_sem=tile_send, recv_sem=tile_recv,
             device_id=device(step // nf, 0, lax.rem(step, nf)), device_id_type=MESH,
         ).start()
 
@@ -269,20 +289,17 @@
             send_sem=rows_send, recv_sem=rows_recv, device_id=device(0, step, 0), device_id_type=MESH,
         ).start()
 
-    other_tiles = tiles_in.at[pl.ds(0, nc * nf - 1)]
-    other_clips = rows_in.at[pl.ds(0, nv - 1)]
-    pltpu.make_async_copy(other_tiles, other_tiles, tile_recv).wait()
-    all_picked = jnp.sum(tiles_in[...], axis=0)
-    live_share = jnp.where(live, all_picked, 0.0)
-    own_logits = logit_scale * (times_exact(live_share, same_group) / safe_length)
-    logit_tile = jnp.where((slot_in_group == me_v) & used, own_logits, 0.0)
-    tile_out[1] = logit_tile
-    logits_in[me_v] = logit_tile
+    other_scores = scores_in.at[pl.ds(0, nc * nf - 1)]
+    pltpu.make_async_copy(other_scores, other_scores, score_recv).wait()
+    own_logits = jnp.sum(scores_in[...], axis=0, keepdims=True)
+    line_out[1:2, :] = own_logits
+    own_line = pl.ds(me_v, 1)
+    logits_in[own_line, :] = own_logits
 
     @pl.loop(1, nv)
     def _(step):
         pltpu.make_async_remote_copy(
-            src_ref=tile_out.at[1], dst_ref=logits_in.at[me_v], send_sem=logit_send, recv_sem=logit_recv,
+            src_ref=line_out.at[1:2], dst_ref=logits_in.at[own_line], send_sem=logit_send, recv_sem=logit_recv,
             device_id=device(0, step, 0), device_id_type=MESH,
         ).start()
 
@@ -299,26 +316,36 @@
     for copy in spreads:
         copy.start()
 
+    other_tiles = tiles_in.at[pl.ds(0, nc * nf - 1)]
+    other_clips = rows_in.at[pl.ds(0, nv - 1)]
+    pltpu.make_async_copy(other_tiles, other_tiles, tile_recv).wait()
+    live_share = jnp.where(live, jnp.sum(tiles_in[...], axis=0), 0.0)
     share_row = as_row(times_exact(live_share / safe_length, spread_table[...]))
     share_high, share_low = two_terms(one_hot[...].astype(f32) * share_row)
     inner_table = dot(share_high, caption_table[...]) + dot(share_low, caption_table[...])
     pltpu.make_async_copy(other_clips, other_clips, rows_recv).wait()
 
-    pltpu.make_async_copy(other_clips, other_clips, logit_recv).wait()
-    logits = jnp.sum(logits_in[...], axis=0)
-    exp_logits = jnp.where(used, jnp.exp(logits), 0.0)
-    row_total = times_exact(exp_logits, same_group)
-    col = jnp.broadcast_to(jnp.sum(exp_logits, axis=0, keepdims=True), (SUB, LANES))
-    col_total = col
-    for j in range(1, LANES // tok):
-        col_total = col_total + pltpu.roll(col, j * tok, 1)
-    positive = jnp.where(used & (slot_in_group == group * SUB + sub), 1.0, 0.0)
-    grad = logit_scale * (0.5 * (exp_logits / row_total + exp_logits / col_total) - positive)
-    weight = jnp.where(used, grad / safe_length, 0.0)
-
-    block_weight = jnp.zeros((SUB, LANES), f32)
-    for j in range(nc):
-        block_weight = jnp.where(me_c == j, pltpu.roll(weight, (LANES - j * tok) % LANES, 1), block_weight)
+    length_line = jnp.zeros((SUB, LANES), f32)
+    for j in range(nc):
+        length_line = jnp.where(lane == j * cap_lanes + sub, trade[j, 3 * SUB : 4 * SUB, :], length_line)
+    inverse_length = 1.0 / jnp.maximum(jnp.sum(length_line, axis=0, keepdims=True), 1.0)
+    clip_id = iota((nv, LANES), 0)
+    line_lane = iota((nv, LANES), 1)
+    valid = (line_lane & (cap_lanes - 1)) < SUB
+    positive = valid & (clip_id == group_of(line_lane, cap_lanes) * SUB + (line_lane & (cap_lanes - 1)))
+    positive = positive.astype(f32)
+
+    other_logits = logits_in.at[pl.ds(0, nv - 1)]
+    pltpu.make_async_copy(other_logits, other_logits, logit_recv).wait()
+    logits = logits_in[...]
+    exp_logits = jnp.where(valid, jnp.exp(logits), 0.0)
+    row_total = jnp.where(in_line[0:1], jnp.sum(exp_logits, axis=0, keepdims=True), 1.0)
+    col_total = jnp.sum(exp_logits, axis=1, keepdims=True)
+    grad = logit_scale * (exp_logits * (0.5 / row_total + 0.5 / col_total) - positive)
+    weights[...] = grad
+    turned[...] = jnp.transpose(grad * inverse_length)
+
+    block_weight = turned[pl.ds(pl.multiple_of(me_c * cap_lanes, SUB), SUB), :]
     slice_grad = jnp.zeros((SUB, LANES), f32)
     for v in range(nv):
         slice_grad = slice_grad + block_weight[:, v : v + 1] * rows_in[v]
@@ -336,17 +363,14 @@
     for copy in grad_copies:
         copy.start()
 
-    own = jnp.where(slot_in_group == me_v, grad, 0.0)
-    row_weight = jnp.zeros((SUB, LANES), f32)
-    token_weight = []
-    for j in range(nc):
-        value = jnp.sum(jnp.where(group == j, own, 0.0), axis=1, keepdims=True)
-        row_weight = jnp.where(lane == j * (LANES // nc) + sub, value, row_weight)
-        token_weight.append(value / jnp.maximum(trade[j, 3 * SUB : 4 * SUB, :], 1.0))
-    inner = jnp.sum(inner_table * jnp.sum(row_weight, axis=0, keepdims=True), axis=1, keepdims=True)
+    own_grad = weights[own_line, :]
+    own_weight = own_grad * inverse_length
+    token_weight = [
+        jnp.sum(jnp.where(lane == j * cap_lanes + sub, own_weight, 0.0), axis=1, keepdims=True) for j in range(nc)
+    ]
+    inner = jnp.sum(inner_table * own_grad, axis=1, keepdims=True)
     for copy in spreads:
         copy.wait()
-    when = iota((tok, SUB, LANES), 0).astype(f32)
     parts = []
     for j in range(nc):
         mask = when < trade[j, 3 * SUB : 4 * SUB, :][None]
@@ -354,13 +378,10 @@
         parts.append(jnp.concatenate(two_terms(scaled.reshape(per_block, LANES)), axis=1))
     both = dot(one_hot[...], jnp.concatenate(parts, axis=0))
     clip_res[...] = key_inv[...] * (both[:, 0:LANES] + both[:, LANES:] - unit_keys[me_c] * inner)
-    clip_store = pltpu.make_async_copy(clip_res, clip_out, store_sem.at[0])
-    clip_store.start()
-
-    terms = jnp.where((slot_in_group == 0) & used, jnp.log(row_total), 0.0)
-    terms = terms + jnp.where((lane < tok) & (sub == 0), jnp.log(col_total), 0.0)
-    terms = 0.5 * terms - positive * logits
-    loss_ref[0, 0] = jnp.sum(terms) / (nc * SUB)
+
+    terms = 0.5 * jnp.sum(jnp.where(in_line[0:1], jnp.log(row_total), 0.0)) + 0.5 * jnp.sum(jnp.log(col_total))
+    terms = terms - jnp.sum(positive * logits)
+    loss_ref[...] = jnp.broadcast_to(terms / (nc * SUB), (1, 1))
 
     for copy in grad_copies:
         copy.wait()
@@ -370,16 +391,13 @@
     cap_inner = jnp.sum(dot_tile, axis=1, keepdims=True)
     for j in range(nc):
         cap_res[pl.ds(j, SUB, stride=nc), :] = cap_inv * (grads_in[j] - qn[j] * cap_inner)
-    cap_store = pltpu.make_async_copy(cap_res, cap_out, store_sem.at[1])
-    cap_store.start()
 
     pltpu.make_async_copy(gathered, gathered, pick_send).wait()
     pltpu.make_async_copy(gathered, gathered, gather_send).wait()
     pltpu.make_async_copy(other_clips, other_clips, rows_send).wait()
-    pltpu.make_async_copy(other_clips, other_clips, logit_send).wait()
+    pltpu.make_async_copy(other_scores, other_scores, score_send).wait()
+    pltpu.make_async_copy(other_logits, other_logits, logit_send).wait()
     pltpu.make_async_copy(other_tiles, other_tiles, tile_send).wait()
-    clip_store.wait()
-    cap_store.wait()
 
 
 def body(nc, nv, cap_tokens, clip_tokens, win_frame, win_patch, cap_lengths):
@@ -411,38 +429,40 @@
         vmem((per_block, LANES), f32),
         vmem((nv, SUB, LANES), f32),
         vmem((nc * nc, SUB, LANES), f32),
-        vmem((nv, SUB, LANES), f32),
-        vmem((2, SUB, LANES), f32),
+        vmem((nc * nc, LANES), f32),
+        vmem((nv, LANES), f32),
+        vmem((SUB, LANES), f32),
+        vmem((SUB, LANES), f32),
+        vmem((nv, LANES), f32),
+        vmem((LANES, nv), f32),
         vmem((nc, SUB, LANES), f32),
         vmem((SUB, LANES), f32),
         vmem((LANES, nc * per_block), bf16),
         vmem((nc * per_block, LANES), bf16),
         vmem((rows, nc * per_block), bf16),
-        vmem((SUB * nc, LANES), f32),
-        vmem((rows, LANES), f32),
-        dma((4,)), dma((2,)),
+        vmem((1, SUB), jnp.int32),
+        dma((5,)),
         dma((nc,)), dma((nc,)), dma((nc,)), dma((nc,)),
         dma, dma, dma, dma,
         dma((nc,)), dma((nc,)),
-        dma, dma, dma, dma, dma, dma,
+        dma, dma, dma, dma, dma, dma, dma, dma,
         dma((nc,)), dma((nc,)),
     ]
     hbm = pl.BlockSpec(memory_space=pl.ANY)
-    smem = pl.BlockSpec(memory_space=pltpu.SMEM)
+    near = pl.BlockSpec(memory_space=pltpu.VMEM)
+    in_hbm = functools.partial(pltpu.with_memory_space_constraint, memory_space=pltpu.HBM)
+    operands = (caps, clips, win_frame.reshape(SUB, nv), win_patch.reshape(SUB, nv), cap_lengths.reshape(1, SUB))
+    shapes = ((1, 1), (SUB * nc, LANES), (rows, LANES))
     loss, cap_grad, clip_grad = pl.pallas_call(
         functools.partial(kernel, nc, nv, patches),
-        out_shape=(
-            jax.ShapeDtypeStruct((1, 1), f32),
-            jax.ShapeDtypeStruct((SUB * nc, LANES), f32),
-            jax.ShapeDtypeStruct((rows, LANES), f32),
-        ),
-        in_specs=[hbm, hbm, hbm, hbm, smem],
-        out_specs=(smem, hbm, hbm),
+        out_shape=[vmem(shape, f32) for shape in shapes],
+        in_specs=[hbm] * 5,
+        out_specs=[near] * 3,
         scratch_shapes=scratch,
         compiler_params=pltpu.CompilerParams(
-            collective_id=0, has_side_effects=True, vmem_limit_bytes=60 * 1024 * 1024
+            collective_id=0, has_side_effects=True, vmem_limit_bytes=32 * 1024 * 1024
         ),
-    )(caps, clips, win_frame.reshape(SUB, nv), win_patch.reshape(SUB, nv), cap_lengths)
+    )(*map(in_hbm, operands))
     clip_grad = clip_grad.reshape(patches, frames, LANES).transpose(1, 0, 2)[None]
     return loss.reshape(()), cap_grad.reshape(SUB, 1, width), clip_grad
 

time: 52.8 us -> 45.2 us (0.86)
  Pallas kernels: 47.2 us -> 42 us
  local copies, waits for them, and re-layouts: 2.87 us -> 1.25 us
  between operations: 2.45 us -> 1.8 us
    pallas_call x1, Pallas kernels: 47.2 us -> 42 us  [body(): pl.pallas_call(functools.partial(kernel, nc, nv, patches), out_shape=[vme...]
    unnamed x2, local copies, waits for them, and re-layouts: 2.87 us -> 1.25 us
where the time goes in v3:
time: 45.2 us; the launch traced here: 45.1 us
  Pallas kernels  42 us (93%)
  between operations  1.8 us (4%)
  local copies, waits for them, and re-layouts  1.25 us (3%)
    pallas_call x1, Pallas kernels, body(): pl.pallas_call(functools.partial(kernel, nc, nv, patches), out_shape=[vme...  42 us
    unnamed x2, local copies, waits for them, and re-layouts  1.25 us

profile of v3, /device:TPU:1, one launch (start us, length us, event | category | flops | bytes accessed | tf_op | source)
XLA Modules:
  0.0 45.1 jit_solution(10790756005573764935)
XLA Ops:
  0.6 42.0 %shard_map.76 = (f32[1,1]{1,0:T(1,128)S(1)}, f32[32,128]{1,0:T(8,128)S(1)}, f32[200,128]{1,0:T(8,128)S(1)}) custom-call(f32[32,128]{1,0:T(8,128)} %bitcast.19, f32[50,16,128]{2,1,0:T(8,128)} %bitcast.18, s32[8,32]{1,0:T(8,128)} %bitcast.20, s32[8,32]{1,0:T(8,128)} %bitcast.21, s32[1,8]{1,0:T(1,128)} %bitcast.22), custom_call_target="tpu_custom_call" | custom-call | tf_op jit(solution)/shard_map/pallas_call | solution.py:456
  42.7 0.6 %copy.14 = f32[8,1,512]{2,1,0:T(1,128)} copy(f32[8,1,512]{2,1,0:T(1,128)S(1)} %bitcast.17) | data formatting | bytes 32768
  43.3 0.6 %copy.15 = f32[1,4,50,128]{3,1,2,0:T(4,128)} copy(f32[1,4,50,128]{3,1,2,0:T(4,128)S(1)} %bitcast.16) | data formatting | bytes 204800

commit v4 on v3

--- a/solution.py
+++ b/solution.py
@@ -57,7 +57,7 @@
     cap_ref, clip_ref, wf_ref, wp_ref, len_ref,
     loss_ref, cap_res, clip_res,
     cap_raw, clip_raw, wf_raw, wp_raw, qn, give, trade, q_full, q_pick, unit_keys, keys, key_inv, key_cat, column,
-    picked_rows, rows_in, tiles_in, scores_in, logits_in, tile_out, line_out, weights, turned, grads_in, grad_out, spread_table, caption_table, one_hot,
+    picked_rows, rows_in, tiles_in, scores_in, logits_in, tile_out, line_out, lines_out, weights, turned, grads_in, grad_out, spread_table, caption_table, one_hot,
     len_raw,
     load_sem, trade_send, trade_recv, key_send, key_recv, pick_send, pick_recv, gather_send, gather_recv,
     spread_send, spread_recv, rows_send, rows_recv, tile_send, tile_recv, score_send, score_recv, logit_send, logit_recv, grad_send, grad_recv,
@@ -70,6 +70,12 @@
     per_block = tok * SUB
     all_tokens = nf * per_block
     tok_bits, block_bits = log2(tok), log2(per_block)
+
+    half_clips, side_rows = nv // 2, nv // 4
+    me_half, me_side = me_v // half_clips, lax.rem(me_v, 2)
+    me_row = lax.rem(me_v, half_clips) // 2
+    me_corner = me_half * 2 + me_side
+    others_in_row, others_in_corner = nf * side_rows - 1, nc * 4 - 1
 
     loads = [
         pltpu.make_async_copy(clip_ref, clip_raw, load_sem.at[0]),
@@ -254,22 +260,28 @@
     when = iota((tok, SUB, LANES), 0).astype(f32)
     score = jnp.sum(jnp.sum(jnp.where(when < lengths[None], product, 0.0), axis=0), axis=1, keepdims=True)
     score = score * logit_scale / lengths
-    me_16 = me_c * nf + me_f
-    own_score = pl.ds(me_16, 1)
-    line_out[0:1, :] = jnp.sum(jnp.where(lane == me_c * cap_lanes + sub, score, 0.0), axis=0, keepdims=True)
-    scores_in[own_score, :] = line_out[0:1, :]
-
-    @pl.loop(1, nc * nf)
-    def _(step):
+    own_score = pl.ds(me_f * side_rows + me_row, 1)
+    line_out[...] = jnp.sum(jnp.where(lane == me_c * cap_lanes + sub, score, 0.0), axis=0, keepdims=True)
+    scores_in[own_score, :] = line_out[...]
+
+    @pl.loop(1, nf * side_rows)
+    def _(step):
+        to_row = lax.rem(me_row + step // nf, side_rows)
+        to = {
+            "cap": me_c,
+            "clip": me_half * half_clips + to_row * 2 + me_side,
+            "frame": lax.rem(me_f + lax.rem(step, nf), nf),
+        }
         pltpu.make_async_remote_copy(
-            src_ref=line_out.at[0:1], dst_ref=scores_in.at[own_score], send_sem=score_send, recv_sem=score_recv,
-            device_id=device(step // nf, 0, lax.rem(step, nf)), device_id_type=MESH,
+            src_ref=line_out, dst_ref=scores_in.at[own_score], send_sem=score_send, recv_sem=score_recv,
+            device_id=to, device_id_type=MESH,
         ).start()
 
     tile = jnp.zeros((SUB, LANES), f32)
     for t in range(tok):
         tile = jnp.where(lane == me_c * tok + t, jnp.sum(product[t], axis=1, keepdims=True), tile)
     tile_out[...] = tile
+    me_16 = me_c * nf + me_f
     tiles_in[me_16] = tile
 
     @pl.loop(1, nc * nf)
@@ -289,18 +301,27 @@
             send_sem=rows_send, recv_sem=rows_recv, device_id=device(0, step, 0), device_id_type=MESH,
         ).start()
 
-    other_scores = scores_in.at[pl.ds(0, nc * nf - 1)]
+    other_scores = scores_in.at[pl.ds(0, others_in_row)]
     pltpu.make_async_copy(other_scores, other_scores, score_recv).wait()
-    own_logits = jnp.sum(scores_in[...], axis=0, keepdims=True)
-    line_out[1:2, :] = own_logits
-    own_line = pl.ds(me_v, 1)
-    logits_in[own_line, :] = own_logits
-
-    @pl.loop(1, nv)
-    def _(step):
+    column_logits = scores_in[0:side_rows, :]
+    for j in range(1, nf):
+        column_logits = column_logits + scores_in[j * side_rows : (j + 1) * side_rows, :]
+    lines_out[...] = column_logits
+    own_slot = me_c * 4 + me_corner
+    logits_in[own_slot] = column_logits
+
+    @pl.loop(1, nc * 4)
+    def _(step):
+        corner = lax.rem(step, 4)
+        to_half, to_side = lax.rem(me_half + corner // 2, 2), lax.rem(me_side + lax.rem(corner, 2), 2)
+        to = {
+            "cap": lax.rem(me_c + step // 4, nc),
+            "clip": to_half * half_clips + me_row * 2 + to_side,
+            "frame": me_f,
+        }
         pltpu.make_async_remote_copy(
-            src_ref=line_out.at[1:2], dst_ref=logits_in.at[own_line], send_sem=logit_send, recv_sem=logit_recv,
-            device_id=device(0, step, 0), device_id_type=MESH,
+            src_ref=lines_out, dst_ref=logits_in.at[own_slot], send_sem=logit_send, recv_sem=logit_recv,
+            device_id=to, device_id_type=MESH,
         ).start()
 
     gathered = q_full.at[0, all_but_one]
@@ -329,15 +350,20 @@
     for j in range(nc):
         length_line = jnp.where(lane == j * cap_lanes + sub, trade[j, 3 * SUB : 4 * SUB, :], length_line)
     inverse_length = 1.0 / jnp.maximum(jnp.sum(length_line, axis=0, keepdims=True), 1.0)
-    clip_id = iota((nv, LANES), 0)
+    place = iota((nv, LANES), 0)
+    corner, row = group_of(place, side_rows), place & (side_rows - 1)
+    clip_id = (corner >> 1) * half_clips + row * 2 + (corner & 1)
     line_lane = iota((nv, LANES), 1)
     valid = (line_lane & (cap_lanes - 1)) < SUB
     positive = valid & (clip_id == group_of(line_lane, cap_lanes) * SUB + (line_lane & (cap_lanes - 1)))
     positive = positive.astype(f32)
 
-    other_logits = logits_in.at[pl.ds(0, nv - 1)]
+    other_logits = logits_in.at[pl.ds(0, others_in_corner)]
     pltpu.make_async_copy(other_logits, other_logits, logit_recv).wait()
-    logits = logits_in[...]
+    logits = logits_in[0:4]
+    for j in range(1, nc):
+        logits = logits + logits_in[4 * j : 4 * j + 4]
+    logits = logits.reshape(nv, LANES)
     exp_logits = jnp.where(valid, jnp.exp(logits), 0.0)
     row_total = jnp.where(in_line[0:1], jnp.sum(exp_logits, axis=0, keepdims=True), 1.0)
     col_total = jnp.sum(exp_logits, axis=1, keepdims=True)
@@ -348,7 +374,8 @@
     block_weight = turned[pl.ds(pl.multiple_of(me_c * cap_lanes, SUB), SUB), :]
     slice_grad = jnp.zeros((SUB, LANES), f32)
     for v in range(nv):
-        slice_grad = slice_grad + block_weight[:, v : v + 1] * rows_in[v]
+        at = (v // half_clips * 2 + v % 2) * side_rows + v % half_clips // 2
+        slice_grad = slice_grad + block_weight[:, at : at + 1] * rows_in[v]
     slice_grad = jnp.where(me_v.astype(f32) < lengths, slice_grad, 0.0)
     grad_out[...] = slice_grad
     grads_in[me_f] = slice_grad
@@ -363,7 +390,7 @@
     for copy in grad_copies:
         copy.start()
 
-    own_grad = weights[own_line, :]
+    own_grad = weights[pl.ds(me_corner * side_rows + me_row, 1), :]
     own_weight = own_grad * inverse_length
     token_weight = [
         jnp.sum(jnp.where(lane == j * cap_lanes + sub, own_weight, 0.0), axis=1, keepdims=True) for j in range(nc)
@@ -429,10 +456,11 @@
         vmem((per_block, LANES), f32),
         vmem((nv, SUB, LANES), f32),
         vmem((nc * nc, SUB, LANES), f32),
-        vmem((nc * nc, LANES), f32),
-        vmem((nv, LANES), f32),
+        vmem((nc * nv // 4, LANES), f32),
+        vmem((nc * 4, nv // 4, LANES), f32),
         vmem((SUB, LANES), f32),
-        vmem((SUB, LANES), f32),
+        vmem((1, LANES), f32),
+        vmem((nv // 4, LANES), f32),
         vmem((nv, LANES), f32),
         vmem((LANES, nv), f32),
         vmem((nc, SUB, LANES), f32),

time: 45.2 us -> 43.5 us (0.962)
  Pallas kernels: 42 us -> 40.3 us
    pallas_call x1, Pallas kernels: 42 us -> 40.3 us  [body(): pl.pallas_call(functools.partial(kernel, nc, nv, patches), out_shape=[vme...]
where the time goes in v4:
time: 43.5 us; the launch traced here: 43.3 us
  Pallas kernels  40.3 us (93%)
  between operations  1.8 us (4%)
  local copies, waits for them, and re-layouts  1.25 us (3%)
    pallas_call x1, Pallas kernels, body(): pl.pallas_call(functools.partial(kernel, nc, nv, patches), out_shape=[vme...  40.3 us
    unnamed x2, local copies, waits for them, and re-layouts  1.25 us

profile of v4, /device:TPU:1, one launch (start us, length us, event | category | flops | bytes accessed | tf_op | source)
XLA Modules:
  0.0 43.3 jit_solution(4443789181170965850)
XLA Ops:
  0.6 40.3 %shard_map.76 = (f32[1,1]{1,0:T(1,128)S(1)}, f32[32,128]{1,0:T(8,128)S(1)}, f32[200,128]{1,0:T(8,128)S(1)}) custom-call(f32[32,128]{1,0:T(8,128)} %bitcast.19, f32[50,16,128]{2,1,0:T(8,128)} %bitcast.18, s32[8,32]{1,0:T(8,128)} %bitcast.20, s32[8,32]{1,0:T(8,128)} %bitcast.21, s32[1,8]{1,0:T(1,128)} %bitcast.22), custom_call_target="tpu_custom_call" | custom-call | tf_op jit(solution)/shard_map/pallas_call | solution.py:484
  41.0 0.6 %copy.14 = f32[8,1,512]{2,1,0:T(1,128)} copy(f32[8,1,512]{2,1,0:T(1,128)S(1)} %bitcast.17) | data formatting | bytes 32768
  41.6 0.6 %copy.15 = f32[1,4,50,128]{3,1,2,0:T(4,128)} copy(f32[1,4,50,128]{3,1,2,0:T(4,128)S(1)} %bitcast.16) | data formatting | bytes 204800

commit v5 on v4

--- a/solution.py
+++ b/solution.py
@@ -56,7 +56,7 @@
     nc, nv, patches,
     cap_ref, clip_ref, wf_ref, wp_ref, len_ref,
     loss_ref, cap_res, clip_res,
-    cap_raw, clip_raw, wf_raw, wp_raw, qn, give, trade, q_full, q_pick, unit_keys, keys, key_inv, key_cat, column,
+    cap_raw, clip_raw, wf_raw, wp_raw, qn, give, trade, q_full, q_pick, unit_keys, keys, key_inv, column,
     picked_rows, rows_in, tiles_in, scores_in, logits_in, tile_out, line_out, lines_out, weights, turned, grads_in, grad_out, spread_table, caption_table, one_hot,
     len_raw,
     load_sem, trade_send, trade_recv, key_send, key_recv, pick_send, pick_recv, gather_send, gather_recv,
@@ -66,7 +66,6 @@
     tok = nv
     me_c, me_v, me_f = lax.axis_index("cap"), lax.axis_index("clip"), lax.axis_index("frame")
     rows = 4 * patches
-    all_rows = nf * rows
     per_block = tok * SUB
     all_tokens = nf * per_block
     tok_bits, block_bits = log2(tok), log2(per_block)
@@ -84,9 +83,6 @@
         pltpu.make_async_copy(wp_ref, wp_raw, load_sem.at[3]),
         pltpu.make_async_copy(len_ref, len_raw, load_sem.at[4]),
     ]
-    for load in loads:
-        load.start()
-
     barrier = pltpu.get_barrier_semaphore()
 
     def device(dc, dv, df):
@@ -99,13 +95,20 @@
     def signal(dc, dv, df):
         pl.semaphore_signal(barrier, inc=1, device_id=device(dc, dv, df), device_id_type=MESH)
 
-    @pl.loop(1, nc * nf)
-    def _(step):
-        signal(step // nf, 0, lax.rem(step, nf))
-
-    @pl.loop(1, nv)
-    def _(step):
-        signal(0, step, 0)
+    def at_clip(clip):
+        return {"cap": me_c, "clip": clip, "frame": me_f}
+
+    across = lax.rem(me_v + half_clips, nv)
+    in_half = [me_half * half_clips + lax.rem(me_v + step, half_clips) for step in range(1, half_clips)]
+    pl.semaphore_signal(barrier, inc=1, device_id=at_clip(across), device_id_type=MESH)
+    for clip in in_half:
+        pl.semaphore_signal(barrier, inc=1, device_id=at_clip(clip), device_id_type=MESH)
+    for load in loads:
+        load.start()
+    for step in range(1, nf):
+        signal(0, 0, step)
+    for step in range(1, nc):
+        signal(step, 0, 0)
 
     lane = iota((SUB, LANES), 1)
     sub = iota((SUB, LANES), 0)
@@ -126,6 +129,44 @@
         qn[j] = unit
         give[j, 0:SUB, :] = unit
 
+    for load in loads[2:]:
+        load.wait()
+    diagonal = iota((SUB, SUB), 0) == iota((SUB, SUB), 1)
+    lengths = jnp.sum(jnp.where(diagonal, len_raw[...].astype(f32), 0.0), axis=1, keepdims=True)
+    lengths = jnp.broadcast_to(lengths, (SUB, LANES))
+    give[:, SUB : 3 * SUB, :] = jnp.zeros((nc, 2 * SUB, LANES), f32)
+    for j in range(nc):
+        give[j, SUB : 2 * SUB, 0:tok] = wf_raw[...].astype(f32)
+        give[j, 2 * SUB : 3 * SUB, 0:tok] = wp_raw[...].astype(f32)
+        give[j, 3 * SUB : 4 * SUB, :] = lengths
+
+    pl.semaphore_wait(barrier, nc - 1 + nf - 1 + half_clips)
+
+    own_rows = pl.ds(pl.multiple_of(me_v * SUB, SUB), SUB)
+
+    def pick_copy(src, place, clip, sem):
+        return pltpu.make_async_remote_copy(
+            src_ref=src, dst_ref=q_pick.at[place], send_sem=pick_send.at[sem], recv_sem=pick_recv.at[sem],
+            device_id=at_clip(clip), device_id_type=MESH,
+        )
+
+    across_copy = pick_copy(qn.at[me_f], own_rows, across, 0)
+    across_copy.start()
+    for clip in in_half:
+        pick_copy(qn.at[me_f], own_rows, clip, 1).start()
+
+    def trade_copy(d):
+        to = lax.rem(me_c + d, nc)
+        return pltpu.make_async_remote_copy(
+            src_ref=give.at[to], dst_ref=trade.at[me_c], send_sem=trade_send.at[d], recv_sem=trade_recv.at[d],
+            device_id=device(d, 0, 0), device_id_type=MESH,
+        )
+
+    trades = [trade_copy(d) for d in range(1, nc)]
+    for copy in trades:
+        copy.start()
+
+    keys[:, rows:, :] = jnp.zeros((nf, keys.shape[1] - rows, LANES), f32)
     loads[0].wait()
     whole = clip_raw[...].reshape(patches, nc // 2, SUB, LANES)
     square = whole * whole
@@ -143,14 +184,10 @@
     inverse = jnp.broadcast_to(inverse, (patches, SUB, LANES)).reshape(patches // 2, 2, SUB, LANES)
     key_inv[...] = jnp.where(low_half, inverse[:, 0], inverse[:, 1]).reshape(rows, LANES)
 
-    pl.semaphore_wait(barrier, nc * nf - 1 + nv - 1)
-
-    own_key_rows = pl.ds(pl.multiple_of(me_f * rows, SUB), rows)
-    own_rows = pl.ds(pl.multiple_of(me_v * SUB, SUB), SUB)
 
     def key_copy(d):
         return pltpu.make_async_remote_copy(
-            src_ref=unit_keys.at[lax.rem(me_f + d, nf)], dst_ref=keys.at[own_key_rows],
+            src_ref=unit_keys.at[lax.rem(me_f + d, nf)], dst_ref=keys.at[me_f, pl.ds(0, rows)],
             send_sem=key_send.at[d], recv_sem=key_recv.at[d], device_id=device(0, 0, d), device_id_type=MESH,
         )
 
@@ -158,50 +195,25 @@
     for copy in key_copies:
         copy.start()
 
-    @pl.loop(1, nv)
-    def _(step):
-        pltpu.make_async_remote_copy(
-            src_ref=qn.at[me_f], dst_ref=q_pick.at[own_rows],
-            send_sem=pick_send, recv_sem=pick_recv, device_id=device(0, step, 0), device_id_type=MESH,
-        ).start()
-
-    for load in loads[2:]:
-        load.wait()
-    diagonal = iota((SUB, SUB), 0) == iota((SUB, SUB), 1)
-    lengths = jnp.sum(jnp.where(diagonal, len_raw[...].astype(f32), 0.0), axis=1, keepdims=True)
-    lengths = jnp.broadcast_to(lengths, (SUB, LANES))
-    give[:, SUB : 3 * SUB, :] = jnp.zeros((nc, 2 * SUB, LANES), f32)
-    for j in range(nc):
-        give[j, SUB : 2 * SUB, 0:tok] = wf_raw[...].astype(f32)
-        give[j, 2 * SUB : 3 * SUB, 0:tok] = wp_raw[...].astype(f32)
-        give[j, 3 * SUB : 4 * SUB, :] = lengths
-
-    def trade_copy(d):
-        to = lax.rem(me_c + d, nc)
-        return pltpu.make_async_remote_copy(
-            src_ref=give.at[to], dst_ref=trade.at[me_c], send_sem=trade_send.at[d], recv_sem=trade_recv.at[d],
-            device_id=device(d, 0, 0), device_id_type=MESH,
-        )
-
-    trades = [trade_copy(d) for d in range(1, nc)]
-    for copy in trades:
-        copy.start()
     trade[me_c] = give[me_c]
-    keys[own_key_rows, :] = unit_keys[me_f]
+    keys[me_f, 0:rows, :] = unit_keys[me_f]
     q_pick[own_rows, :] = qn[me_f]
 
     frame_own = wf_raw[...]
-    winner = (frame_own >> 2) * rows + wp_raw[...] * 4 + (frame_own & 3)
+    chunk = keys.shape[1]
+    winner = (frame_own >> 2) * chunk + wp_raw[...] * 4 + (frame_own & 3)
     for t in range(tok):
         column[t * SUB : (t + 1) * SUB, :] = jnp.broadcast_to(winner[:, t : t + 1], (SUB, LANES))
-    wide_lane = iota((per_block, LANES), 1)
-    column_value = column[...]
-    padded = key_cat.shape[0]
-    chosen = jnp.concatenate(
-        [(column_value == wide_lane + k * LANES).astype(f32).astype(bf16) for k in range(padded // LANES)], axis=1
-    )
-    if padded > all_rows:
-        key_cat[all_rows:padded, :] = jnp.zeros((padded - all_rows, 2 * LANES), bf16)
+    wide_lane = iota((per_block, chunk), 1)
+    column_value = jnp.concatenate([column[...]] * (chunk // LANES), axis=1)
+
+    def picked_from(d):
+        part = lax.rem(me_f + nf - d, nf)
+        chosen = (column_value == wide_lane + part * chunk).astype(f32).astype(bf16)
+        both = dot(chosen, jnp.concatenate(two_terms(keys[part]), axis=1))
+        return both[:, 0:LANES] + both[:, LANES:]
+
+    picked = picked_from(0)
 
     from_lane = iota((LANES, all_tokens), 0)
     token = iota((LANES, all_tokens), 1)
@@ -217,16 +229,23 @@
     def as_row(values):
         return jnp.sum(jnp.where(mine_of, values, 0.0), axis=0, keepdims=True)
 
+    def gather_copy(clip, to, sem):
+        place = q_full.at[me_f, clip // 2, lax.rem(clip, 2)]
+        return pltpu.make_async_remote_copy(
+            src_ref=place, dst_ref=place, send_sem=gather_send.at[sem], recv_sem=gather_recv.at[sem],
+            device_id=at_clip(to), device_id_type=MESH,
+        )
+
     for copy in trades:
         copy.wait()
-    q_full[me_f, own_rows, :] = trade[me_f, 0:SUB, :]
-
-    @pl.loop(1, nv)
-    def _(step):
-        pltpu.make_async_remote_copy(
-            src_ref=trade.at[me_f, pl.ds(0, SUB)], dst_ref=q_full.at[me_f, own_rows],
-            send_sem=gather_send, recv_sem=gather_recv, device_id=device(0, step, 0), device_id_type=MESH,
-        ).start()
+    q_full[me_f, me_v // 2, me_side] = trade[me_f, 0:SUB, :]
+    across_gather = gather_copy(me_v, across, 0)
+    across_gather.start()
+
+    across_copy.wait()
+    across_rows = pl.ds(pl.multiple_of(across * SUB, SUB), SUB)
+    for clip in in_half:
+        pick_copy(q_pick.at[across_rows], across_rows, clip, 2).start()
 
     frames = jnp.zeros((SUB, LANES), f32)
     patch_all = jnp.zeros((SUB, LANES), f32)
@@ -244,17 +263,20 @@
     local_row = as_row(dot(twice, spread_table[...])[0:SUB]).astype(jnp.int32)
     one_hot[...] = (iota((rows, all_tokens), 0) == local_row).astype(f32).astype(bf16)
 
-    for copy in key_copies:
-        copy.wait()
-    high, low = two_terms(keys[...])
-    key_cat[0:all_rows, 0:LANES] = high
-    key_cat[0:all_rows, LANES:] = low
-    both = dot(chosen, key_cat[...])
-    picked = both[:, 0:LANES] + both[:, LANES:]
+    across_gather.wait()
+    for dr in range(1, side_rows):
+        to = me_half * half_clips + lax.rem(me_row + dr, side_rows) * 2 + me_side
+        gather_copy(me_v, to, 1).start()
+        gather_copy(across, to, 1).start()
+
+    for d in [d for d in range(1, nf) if d != nf // 2] + [nf // 2]:
+        key_copies[d - 1].wait()
+        picked = picked + picked_from(d)
     picked_rows[...] = picked
 
-    all_but_one = pl.ds(0, (nv - 1) * SUB)
-    pltpu.make_async_copy(q_pick.at[all_but_one], q_pick.at[all_but_one], pick_recv).wait()
+    half_but_one = q_pick.at[pl.ds(0, (half_clips - 1) * SUB)]
+    for sem in (1, 2):
+        pltpu.make_async_copy(half_but_one, half_but_one, pick_recv.at[sem]).wait()
     product = (picked * q_pick[...]).reshape(tok, SUB, LANES)
 
     when = iota((tok, SUB, LANES), 0).astype(f32)
@@ -264,13 +286,15 @@
     line_out[...] = jnp.sum(jnp.where(lane == me_c * cap_lanes + sub, score, 0.0), axis=0, keepdims=True)
     scores_in[own_score, :] = line_out[...]
 
-    @pl.loop(1, nf * side_rows)
-    def _(step):
-        to_row = lax.rem(me_row + step // nf, side_rows)
+    def apart(step, size):
+        return min(step, size - step)
+
+    row_steps = [(dr, df) for dr in range(side_rows) for df in range(nf)][1:]
+    for dr, df in sorted(row_steps, key=lambda p: -apart(p[0], side_rows) - apart(p[1], nf)):
         to = {
             "cap": me_c,
-            "clip": me_half * half_clips + to_row * 2 + me_side,
-            "frame": lax.rem(me_f + lax.rem(step, nf), nf),
+            "clip": me_half * half_clips + lax.rem(me_row + dr, side_rows) * 2 + me_side,
+            "frame": lax.rem(me_f + df, nf),
         }
         pltpu.make_async_remote_copy(
             src_ref=line_out, dst_ref=scores_in.at[own_score], send_sem=score_send, recv_sem=score_recv,
@@ -300,6 +324,15 @@
             src_ref=picked_rows.at[pl.ds(pl.multiple_of(to * SUB, SUB), SUB)], dst_ref=rows_in.at[me_v],
             send_sem=rows_send, recv_sem=rows_recv, device_id=device(0, step, 0), device_id_type=MESH,
         ).start()
+
+    row_tiles = q_full.at[0, pl.ds(0, side_rows - 1)]
+    pltpu.make_async_copy(row_tiles, row_tiles, gather_recv.at[1]).wait()
+    side_tiles = q_full.at[me_f, pl.ds(0, half_clips), me_side]
+    side_copy = pltpu.make_async_remote_copy(
+        src_ref=side_tiles, dst_ref=side_tiles, send_sem=gather_send.at[2], recv_sem=gather_recv.at[2],
+        device_id=at_clip(me_v + 1 - 2 * me_side), device_id_type=MESH,
+    )
+    side_copy.start()
 
     other_scores = scores_in.at[pl.ds(0, others_in_row)]
     pltpu.make_async_copy(other_scores, other_scores, score_recv).wait()
@@ -310,12 +343,13 @@
     own_slot = me_c * 4 + me_corner
     logits_in[own_slot] = column_logits
 
-    @pl.loop(1, nc * 4)
-    def _(step):
-        corner = lax.rem(step, 4)
-        to_half, to_side = lax.rem(me_half + corner // 2, 2), lax.rem(me_side + lax.rem(corner, 2), 2)
+    corner_steps = [(dh, ds, dc) for dh in (1, 0) for ds in (0, 1) for dc in range(nc)]
+    for dh, ds, dc in corner_steps:
+        if (dh, ds, dc) == (0, 0, 0):
+            continue
+        to_half, to_side = lax.rem(me_half + dh, 2), lax.rem(me_side + ds, 2)
         to = {
-            "cap": lax.rem(me_c + step // 4, nc),
+            "cap": lax.rem(me_c + dc, nc),
             "clip": to_half * half_clips + me_row * 2 + to_side,
             "frame": me_f,
         }
@@ -324,8 +358,7 @@
             device_id=to, device_id_type=MESH,
         ).start()
 
-    gathered = q_full.at[0, all_but_one]
-    pltpu.make_async_copy(gathered, gathered, gather_recv).wait()
+    side_copy.wait()
 
     def spread_copy(d):
         return pltpu.make_async_remote_copy(
@@ -419,8 +452,9 @@
     for j in range(nc):
         cap_res[pl.ds(j, SUB, stride=nc), :] = cap_inv * (grads_in[j] - qn[j] * cap_inner)
 
-    pltpu.make_async_copy(gathered, gathered, pick_send).wait()
-    pltpu.make_async_copy(gathered, gathered, gather_send).wait()
+    for sem in (1, 2):
+        pltpu.make_async_copy(half_but_one, half_but_one, pick_send.at[sem]).wait()
+    pltpu.make_async_copy(row_tiles, row_tiles, gather_send.at[1]).wait()
     pltpu.make_async_copy(other_clips, other_clips, rows_send).wait()
     pltpu.make_async_copy(other_scores, other_scores, score_send).wait()
     pltpu.make_async_copy(other_logits, other_logits, logit_send).wait()
@@ -433,7 +467,6 @@
     assert block == SUB and frames == 4 and width == nc * LANES and win_frame.shape == (SUB, nv, 1)
     rows = frames * patches
     per_block = nv * SUB
-    padded = -(-nc * rows // LANES) * LANES
     caps = cap_tokens.reshape(SUB * nc, LANES)
     clips = clip_tokens.reshape(frames, patches, nc, LANES).transpose(1, 2, 0, 3).reshape(patches, nc * frames, LANES)
     vmem = pltpu.VMEM
@@ -446,12 +479,11 @@
         vmem((nc, SUB, LANES), f32),
         vmem((nc, 4 * SUB, LANES), f32),
         vmem((nc, 4 * SUB, LANES), f32),
-        vmem((nc, per_block, LANES), f32),
+        vmem((nc, nv // 2, 2, SUB, LANES), f32),
         vmem((per_block, LANES), f32),
         vmem((nc, rows, LANES), f32),
-        vmem((nc * rows, LANES), f32),
+        vmem((nc, -(-rows // LANES) * LANES, LANES), f32),
         vmem((rows, LANES), f32),
-        vmem((padded, 2 * LANES), bf16),
         vmem((per_block, LANES), jnp.int32),
         vmem((per_block, LANES), f32),
         vmem((nv, SUB, LANES), f32),
@@ -471,7 +503,7 @@
         vmem((1, SUB), jnp.int32),
         dma((5,)),
         dma((nc,)), dma((nc,)), dma((nc,)), dma((nc,)),
-        dma, dma, dma, dma,
+        dma((3,)), dma((3,)), dma((3,)), dma((3,)),
         dma((nc,)), dma((nc,)),
         dma, dma, dma, dma, dma, dma, dma, dma,
         dma((nc,)), dma((nc,)),

time: 43.5 us -> 42.2 us (0.970)
  Pallas kernels: 40.3 us -> 39 us
    pallas_call x1, Pallas kernels: 40.3 us -> 39 us  [body(): pl.pallas_call(functools.partial(kernel, nc, nv, patches), out_shape=[vme...]
where the time goes in v5:
time: 42.2 us; the launch traced here: 42.1 us
  Pallas kernels  39 us (92%)
  between operations  1.8 us (4%)
  local copies, waits for them, and re-layouts  1.25 us (3%)
    pallas_call x1, Pallas kernels, body(): pl.pallas_call(functools.partial(kernel, nc, nv, patches), out_shape=[vme...  39 us
    unnamed x2, local copies, waits for them, and re-layouts  1.25 us

profile of v5, /device:TPU:1, one launch (start us, length us, event | category | flops | bytes accessed | tf_op | source)
XLA Modules:
  0.0 42.1 jit_solution(1845736619940668629)
XLA Ops:
  0.6 39.0 %shard_map.76 = (f32[1,1]{1,0:T(1,128)S(1)}, f32[32,128]{1,0:T(8,128)S(1)}, f32[200,128]{1,0:T(8,128)S(1)}) custom-call(f32[32,128]{1,0:T(8,128)} %bitcast.19, f32[50,16,128]{2,1,0:T(8,128)} %bitcast.18, s32[8,32]{1,0:T(8,128)} %bitcast.20, s32[8,32]{1,0:T(8,128)} %bitcast.21, s32[1,8]{1,0:T(1,128)} %bitcast.22), custom_call_target="tpu_custom_call" | custom-call | tf_op jit(solution)/shard_map/pallas_call | solution.py:516
  39.7 0.6 %copy.14 = f32[8,1,512]{2,1,0:T(1,128)} copy(f32[8,1,512]{2,1,0:T(1,128)S(1)} %bitcast.17) | data formatting | bytes 32768
  40.3 0.6 %copy.15 = f32[1,4,50,128]{3,1,2,0:T(4,128)} copy(f32[1,4,50,128]{3,1,2,0:T(4,128)S(1)} %bitcast.16) | data formatting | bytes 204800

commit v6 on v5

--- a/solution.py
+++ b/solution.py
@@ -57,7 +57,7 @@
     cap_ref, clip_ref, wf_ref, wp_ref, len_ref,
     loss_ref, cap_res, clip_res,
     cap_raw, clip_raw, wf_raw, wp_raw, qn, give, trade, q_full, q_pick, unit_keys, keys, key_inv, column,
-    picked_rows, rows_in, tiles_in, scores_in, logits_in, tile_out, line_out, lines_out, weights, turned, grads_in, grad_out, spread_table, caption_table, one_hot,
+    picked_rows, rows_in, tiles_in, scores_in, logits_in, tile_out, line_out, lines_out, weights, turned, grads_in, grad_out, spread_table, sums_table, caption_table, one_hot,
     len_raw,
     load_sem, trade_send, trade_recv, key_send, key_recv, pick_send, pick_recv, gather_send, gather_recv,
     spread_send, spread_recv, rows_send, rows_recv, tile_send, tile_recv, score_send, score_recv, logit_send, logit_recv, grad_send, grad_recv,
@@ -83,6 +83,8 @@
         pltpu.make_async_copy(wp_ref, wp_raw, load_sem.at[3]),
         pltpu.make_async_copy(len_ref, len_raw, load_sem.at[4]),
     ]
+    logits_in[...] = jnp.zeros((4 * SUB, LANES), f32)
+
     barrier = pltpu.get_barrier_semaphore()
 
     def device(dc, dv, df):
@@ -116,7 +118,6 @@
     slot_in_group = lane & (tok - 1)
     used = group < nc
     cap_lanes = LANES // nc
-    in_line = (lane & (cap_lanes - 1)) < SUB
 
     loads[1].wait()
     raw = [cap_raw[pl.ds(j, SUB, stride=nc), :] for j in range(nc)]
@@ -215,6 +216,14 @@
 
     picked = picked_from(0)
 
+    from_row, to_row = iota((LANES, LANES), 0), iota((LANES, LANES), 1)
+    of_caption, of_clip = (from_row & 7) == (to_row & 7), (from_row >> 3) == (to_row >> 3)
+    sums_table[...] = jnp.concatenate([of_caption, of_clip], axis=1).astype(f32).astype(bf16)
+    corner, block, at = (iota((4, SUB, LANES), d) for d in range(3))
+    valid = (block < nc) & (at < side_rows * SUB)
+    clip_id = (corner >> 1) * half_clips + (at >> 3) * 2 + (corner & 1)
+    positive = (valid & (clip_id == block * SUB + (at & 7))).astype(f32)
+
     from_lane = iota((LANES, all_tokens), 0)
     token = iota((LANES, all_tokens), 1)
     spread_table[...] = (
@@ -283,7 +292,7 @@
     score = jnp.sum(jnp.sum(jnp.where(when < lengths[None], product, 0.0), axis=0), axis=1, keepdims=True)
     score = score * logit_scale / lengths
     own_score = pl.ds(me_f * side_rows + me_row, 1)
-    line_out[...] = jnp.sum(jnp.where(lane == me_c * cap_lanes + sub, score, 0.0), axis=0, keepdims=True)
+    line_out[...] = jnp.sum(jnp.where(lane == me_row * SUB + sub, score, 0.0), axis=0, keepdims=True)
     scores_in[own_score, :] = line_out[...]
 
     def apart(step, size):
@@ -336,12 +345,9 @@
 
     other_scores = scores_in.at[pl.ds(0, others_in_row)]
     pltpu.make_async_copy(other_scores, other_scores, score_recv).wait()
-    column_logits = scores_in[0:side_rows, :]
-    for j in range(1, nf):
-        column_logits = column_logits + scores_in[j * side_rows : (j + 1) * side_rows, :]
-    lines_out[...] = column_logits
-    own_slot = me_c * 4 + me_corner
-    logits_in[own_slot] = column_logits
+    lines_out[...] = jnp.sum(scores_in[...], axis=0, keepdims=True)
+    own_slot = pl.ds(me_corner * SUB + me_c, 1)
+    logits_in[own_slot, :] = lines_out[...]
 
     corner_steps = [(dh, ds, dc) for dh in (1, 0) for ds in (0, 1) for dc in range(nc)]
     for dh, ds, dc in corner_steps:
@@ -379,36 +385,30 @@
     inner_table = dot(share_high, caption_table[...]) + dot(share_low, caption_table[...])
     pltpu.make_async_copy(other_clips, other_clips, rows_recv).wait()
 
-    length_line = jnp.zeros((SUB, LANES), f32)
-    for j in range(nc):
-        length_line = jnp.where(lane == j * cap_lanes + sub, trade[j, 3 * SUB : 4 * SUB, :], length_line)
-    inverse_length = 1.0 / jnp.maximum(jnp.sum(length_line, axis=0, keepdims=True), 1.0)
-    place = iota((nv, LANES), 0)
-    corner, row = group_of(place, side_rows), place & (side_rows - 1)
-    clip_id = (corner >> 1) * half_clips + row * 2 + (corner & 1)
-    line_lane = iota((nv, LANES), 1)
-    valid = (line_lane & (cap_lanes - 1)) < SUB
-    positive = valid & (clip_id == group_of(line_lane, cap_lanes) * SUB + (line_lane & (cap_lanes - 1)))
-    positive = positive.astype(f32)
+    length_lines = jnp.zeros((SUB, LANES), f32)
+    for j in range(nc):
+        line = jnp.sum(jnp.where((lane & 7) == sub, trade[j, 3 * SUB : 4 * SUB, :], 0.0), axis=0, keepdims=True)
+        length_lines = jnp.where(sub == j, line, length_lines)
+    inverse_length = 1.0 / jnp.maximum(length_lines, 1.0)
 
     other_logits = logits_in.at[pl.ds(0, others_in_corner)]
     pltpu.make_async_copy(other_logits, other_logits, logit_recv).wait()
-    logits = logits_in[0:4]
-    for j in range(1, nc):
-        logits = logits + logits_in[4 * j : 4 * j + 4]
-    logits = logits.reshape(nv, LANES)
-    exp_logits = jnp.where(valid, jnp.exp(logits), 0.0)
-    row_total = jnp.where(in_line[0:1], jnp.sum(exp_logits, axis=0, keepdims=True), 1.0)
-    col_total = jnp.sum(exp_logits, axis=1, keepdims=True)
+    logits = logits_in[...]
+    exp_logits = jnp.where(valid, jnp.exp(logits).reshape(4, SUB, LANES), 0.0)
+    terms = jnp.concatenate(three_terms(exp_logits.reshape(4 * SUB, LANES)), axis=0).astype(bf16)
+    sums = dot(terms, sums_table[...]).reshape(3, 4, SUB, 2 * LANES)
+    sums = sums[0] + sums[1] + sums[2]
+    row_total = jnp.where(valid[0], jnp.sum(sums[:, :, 0:LANES], axis=0), 1.0)
+    col_total = jnp.where(at[:, 0:1] < side_rows * SUB, jnp.sum(sums[:, :, LANES:], axis=1, keepdims=True), 1.0)
     grad = logit_scale * (exp_logits * (0.5 / row_total + 0.5 / col_total) - positive)
-    weights[...] = grad
-    turned[...] = jnp.transpose(grad * inverse_length)
-
-    block_weight = turned[pl.ds(pl.multiple_of(me_c * cap_lanes, SUB), SUB), :]
+    weights[...] = grad.reshape(4 * SUB, LANES)
+    block_grad = jnp.sum(jnp.where(block == me_c, grad * inverse_length, 0.0), axis=1, keepdims=True)
+    turned[...] = jnp.transpose(jnp.broadcast_to(block_grad, (4, SUB, LANES)).reshape(4 * SUB, LANES))
+
     slice_grad = jnp.zeros((SUB, LANES), f32)
     for v in range(nv):
-        at = (v // half_clips * 2 + v % 2) * side_rows + v % half_clips // 2
-        slice_grad = slice_grad + block_weight[:, at : at + 1] * rows_in[v]
+        of_row, of_corner = v % half_clips // 2 * SUB, (v // half_clips * 2 + v % 2) * SUB
+        slice_grad = slice_grad + turned[of_row : of_row + SUB, of_corner : of_corner + 1] * rows_in[v]
     slice_grad = jnp.where(me_v.astype(f32) < lengths, slice_grad, 0.0)
     grad_out[...] = slice_grad
     grads_in[me_f] = slice_grad
@@ -423,11 +423,14 @@
     for copy in grad_copies:
         copy.start()
 
-    own_grad = weights[pl.ds(me_corner * side_rows + me_row, 1), :]
-    own_weight = own_grad * inverse_length
-    token_weight = [
-        jnp.sum(jnp.where(lane == j * cap_lanes + sub, own_weight, 0.0), axis=1, keepdims=True) for j in range(nc)
-    ]
+    own_lines = weights[pl.ds(pl.multiple_of(me_corner * SUB, SUB), SUB), :]
+    own_grad = jnp.zeros((SUB, LANES), f32)
+    token_weight = []
+    for j in range(nc):
+        value = jnp.sum(jnp.where(lane == me_row * SUB + sub, own_lines[j : j + 1], 0.0), axis=1, keepdims=True)
+        own_grad = jnp.where(lane == j * cap_lanes + sub, value, own_grad)
+        token_weight.append(value / jnp.maximum(trade[j, 3 * SUB : 4 * SUB, :], 1.0))
+    own_grad = jnp.sum(own_grad, axis=0, keepdims=True)
     inner = jnp.sum(inner_table * own_grad, axis=1, keepdims=True)
     for copy in spreads:
         copy.wait()
@@ -439,8 +442,10 @@
     both = dot(one_hot[...], jnp.concatenate(parts, axis=0))
     clip_res[...] = key_inv[...] * (both[:, 0:LANES] + both[:, LANES:] - unit_keys[me_c] * inner)
 
-    terms = 0.5 * jnp.sum(jnp.where(in_line[0:1], jnp.log(row_total), 0.0)) + 0.5 * jnp.sum(jnp.log(col_total))
-    terms = terms - jnp.sum(positive * logits)
+    row_terms = jnp.where((sub < nc) & (lane < SUB), jnp.log(row_total), 0.0)
+    col_terms = jnp.where((at[:, 0:1] & 7) == 0, jnp.log(col_total), 0.0)
+    terms = 0.5 * jnp.sum(row_terms) + 0.5 * jnp.sum(col_terms)
+    terms = terms - jnp.sum(positive * logits.reshape(4, SUB, LANES))
     loss_ref[...] = jnp.broadcast_to(terms / (nc * SUB), (1, 1))
 
     for copy in grad_copies:
@@ -489,15 +494,16 @@
         vmem((nv, SUB, LANES), f32),
         vmem((nc * nc, SUB, LANES), f32),
         vmem((nc * nv // 4, LANES), f32),
-        vmem((nc * 4, nv // 4, LANES), f32),
+        vmem((4 * SUB, LANES), f32),
         vmem((SUB, LANES), f32),
         vmem((1, LANES), f32),
-        vmem((nv // 4, LANES), f32),
-        vmem((nv, LANES), f32),
-        vmem((LANES, nv), f32),
+        vmem((1, LANES), f32),
+        vmem((4 * SUB, LANES), f32),
+        vmem((LANES, 4 * SUB), f32),
         vmem((nc, SUB, LANES), f32),
         vmem((SUB, LANES), f32),
         vmem((LANES, nc * per_block), bf16),
+        vmem((LANES, 2 * LANES), bf16),
         vmem((nc * per_block, LANES), bf16),
         vmem((rows, nc * per_block), bf16),
         vmem((1, SUB), jnp.int32),

time: 42.2 us -> 41.9 us (level)
  no operation moved by 1% of the time
where the time goes in v6:
time: 41.9 us; the launch traced here: 41.8 us
  Pallas kernels  38.8 us (93%)
  between operations  1.8 us (4%)
  local copies, waits for them, and re-layouts  1.25 us (3%)
    pallas_call x1, Pallas kernels, body(): pl.pallas_call(functools.partial(kernel, nc, nv, patches), out_shape=[vme...  38.8 us
    unnamed x2, local copies, waits for them, and re-layouts  1.25 us

profile of v6, /device:TPU:1, one launch (start us, length us, event | category | flops | bytes accessed | tf_op | source)
XLA Modules:
  0.0 41.8 jit_solution(7417980760271010261)
XLA Ops:
  0.6 38.8 %shard_map.76 = (f32[1,1]{1,0:T(1,128)S(1)}, f32[32,128]{1,0:T(8,128)S(1)}, f32[200,128]{1,0:T(8,128)S(1)}) custom-call(f32[32,128]{1,0:T(8,128)} %bitcast.19, f32[50,16,128]{2,1,0:T(8,128)} %bitcast.18, s32[8,32]{1,0:T(8,128)} %bitcast.20, s32[8,32]{1,0:T(8,128)} %bitcast.21, s32[1,8]{1,0:T(1,128)} %bitcast.22), custom_call_target="tpu_custom_call" | custom-call | tf_op jit(solution)/shard_map/pallas_call | solution.py:522
  39.4 0.6 %copy.14 = f32[8,1,512]{2,1,0:T(1,128)} copy(f32[8,1,512]{2,1,0:T(1,128)S(1)} %bitcast.17) | data formatting | bytes 32768
  40.0 0.6 %copy.15 = f32[1,4,50,128]{3,1,2,0:T(4,128)} copy(f32[1,4,50,128]{3,1,2,0:T(4,128)S(1)} %bitcast.16) | data formatting | bytes 204800

commit v7 on v6

--- a/solution.py
+++ b/solution.py
@@ -310,20 +310,6 @@
             device_id=to, device_id_type=MESH,
         ).start()
 
-    tile = jnp.zeros((SUB, LANES), f32)
-    for t in range(tok):
-        tile = jnp.where(lane == me_c * tok + t, jnp.sum(product[t], axis=1, keepdims=True), tile)
-    tile_out[...] = tile
-    me_16 = me_c * nf + me_f
-    tiles_in[me_16] = tile
-
-    @pl.loop(1, nc * nf)
-    def _(step):
-        pltpu.make_async_remote_copy(
-            src_ref=tile_out, dst_ref=tiles_in.at[me_16], send_sem=tile_send, recv_sem=tile_recv,
-            device_id=device(step // nf, 0, lax.rem(step, nf)), device_id_type=MESH,
-        ).start()
-
     rows_in[me_v] = picked_rows[own_rows, :]
 
     @pl.loop(1, nv)
@@ -334,14 +320,33 @@
             send_sem=rows_send, recv_sem=rows_recv, device_id=device(0, step, 0), device_id_type=MESH,
         ).start()
 
+    tile = jnp.zeros((SUB, LANES), f32)
+    for t in range(tok):
+        tile = jnp.where(lane == me_c * tok + t, jnp.sum(product[t], axis=1, keepdims=True), tile)
+    tile_out[...] = tile
+    me_16 = me_c * nf + me_f
+    tiles_in[me_16] = tile
+
+    @pl.loop(1, nc * nf)
+    def _(step):
+        pltpu.make_async_remote_copy(
+            src_ref=tile_out, dst_ref=tiles_in.at[me_16], send_sem=tile_send, recv_sem=tile_recv,
+            device_id=device(step // nf, 0, lax.rem(step, nf)), device_id_type=MESH,
+        ).start()
+
     row_tiles = q_full.at[0, pl.ds(0, side_rows - 1)]
     pltpu.make_async_copy(row_tiles, row_tiles, gather_recv.at[1]).wait()
     side_tiles = q_full.at[me_f, pl.ds(0, half_clips), me_side]
-    side_copy = pltpu.make_async_remote_copy(
-        src_ref=side_tiles, dst_ref=side_tiles, send_sem=gather_send.at[2], recv_sem=gather_recv.at[2],
-        device_id=at_clip(me_v + 1 - 2 * me_side), device_id_type=MESH,
-    )
-    side_copy.start()
+
+    def spread_copy(d):
+        return pltpu.make_async_remote_copy(
+            src_ref=side_tiles, dst_ref=side_tiles, send_sem=spread_send.at[d], recv_sem=spread_recv.at[d],
+            device_id=device(0, 0, d), device_id_type=MESH,
+        )
+
+    spreads = [spread_copy(d) for d in range(1, nf)]
+    for copy in spreads:
+        copy.start()
 
     other_scores = scores_in.at[pl.ds(0, others_in_row)]
     pltpu.make_async_copy(other_scores, other_scores, score_recv).wait()
@@ -364,18 +369,6 @@
             device_id=to, device_id_type=MESH,
         ).start()
 
-    side_copy.wait()
-
-    def spread_copy(d):
-        return pltpu.make_async_remote_copy(
-            src_ref=q_full.at[me_f], dst_ref=q_full.at[me_f], send_sem=spread_send.at[d], recv_sem=spread_recv.at[d],
-            device_id=device(0, 0, d), device_id_type=MESH,
-        )
-
-    spreads = [spread_copy(d) for d in range(1, nf)]
-    for copy in spreads:
-        copy.start()
-
     other_tiles = tiles_in.at[pl.ds(0, nc * nf - 1)]
     other_clips = rows_in.at[pl.ds(0, nv - 1)]
     pltpu.make_async_copy(other_tiles, other_tiles, tile_recv).wait()
@@ -383,6 +376,14 @@
     share_row = as_row(times_exact(live_share / safe_length, spread_table[...]))
     share_high, share_low = two_terms(one_hot[...].astype(f32) * share_row)
     inner_table = dot(share_high, caption_table[...]) + dot(share_low, caption_table[...])
+    for copy in spreads:
+        copy.wait()
+    all_tiles = q_full.at[pl.ds(0, nf), pl.ds(0, half_clips), me_side]
+    side_copy = pltpu.make_async_remote_copy(
+        src_ref=all_tiles, dst_ref=all_tiles, send_sem=gather_send.at[2], recv_sem=gather_recv.at[2],
+        device_id=at_clip(me_v + 1 - 2 * me_side), device_id_type=MESH,
+    )
+    side_copy.start()
     pltpu.make_async_copy(other_clips, other_clips, rows_recv).wait()
 
     length_lines = jnp.zeros((SUB, LANES), f32)
@@ -432,8 +433,7 @@
         token_weight.append(value / jnp.maximum(trade[j, 3 * SUB : 4 * SUB, :], 1.0))
     own_grad = jnp.sum(own_grad, axis=0, keepdims=True)
     inner = jnp.sum(inner_table * own_grad, axis=1, keepdims=True)
-    for copy in spreads:
-        copy.wait()
+    side_copy.wait()
     parts = []
     for j in range(nc):
         mask = when < trade[j, 3 * SUB : 4 * SUB, :][None]

time: 41.9 us -> 41.8 us (level)
  no operation moved by 1% of the time
where the time goes in v7:
time: 41.8 us; the launch traced here: 41.6 us
  Pallas kernels  38.6 us (92%)
  between operations  1.8 us (4%)
  local copies, waits for them, and re-layouts  1.25 us (3%)
    pallas_call x1, Pallas kernels, body(): pl.pallas_call(functools.partial(kernel, nc, nv, patches), out_shape=[vme...  38.6 us
    unnamed x2, local copies, waits for them, and re-layouts  1.25 us

profile of v7, /device:TPU:1, one launch (start us, length us, event | category | flops | bytes accessed | tf_op | source)
XLA Modules:
  0.0 41.6 jit_solution(7982656367945959028)
XLA Ops:
  0.6 38.6 %shard_map.76 = (f32[1,1]{1,0:T(1,128)S(1)}, f32[32,128]{1,0:T(8,128)S(1)}, f32[200,128]{1,0:T(8,128)S(1)}) custom-call(f32[32,128]{1,0:T(8,128)} %bitcast.19, f32[50,16,128]{2,1,0:T(8,128)} %bitcast.18, s32[8,32]{1,0:T(8,128)} %bitcast.20, s32[8,32]{1,0:T(8,128)} %bitcast.21, s32[1,8]{1,0:T(1,128)} %bitcast.22), custom_call_target="tpu_custom_call" | custom-call | tf_op jit(solution)/shard_map/pallas_call | solution.py:522
  39.2 0.6 %copy.14 = f32[8,1,512]{2,1,0:T(1,128)} copy(f32[8,1,512]{2,1,0:T(1,128)S(1)} %bitcast.17) | data formatting | bytes 32768
  39.9 0.6 %copy.15 = f32[1,4,50,128]{3,1,2,0:T(4,128)} copy(f32[1,4,50,128]{3,1,2,0:T(4,128)S(1)} %bitcast.16) | data formatting | bytes 204800

commit v8 on v7

--- a/solution.py
+++ b/solution.py
@@ -406,10 +406,11 @@
     block_grad = jnp.sum(jnp.where(block == me_c, grad * inverse_length, 0.0), axis=1, keepdims=True)
     turned[...] = jnp.transpose(jnp.broadcast_to(block_grad, (4, SUB, LANES)).reshape(4 * SUB, LANES))
 
-    slice_grad = jnp.zeros((SUB, LANES), f32)
+    shares = [jnp.zeros((SUB, LANES), f32)] * 4
     for v in range(nv):
         of_row, of_corner = v % half_clips // 2 * SUB, (v // half_clips * 2 + v % 2) * SUB
-        slice_grad = slice_grad + turned[of_row : of_row + SUB, of_corner : of_corner + 1] * rows_in[v]
+        shares[v % 4] = shares[v % 4] + turned[of_row : of_row + SUB, of_corner : of_corner + 1] * rows_in[v]
+    slice_grad = (shares[0] + shares[1]) + (shares[2] + shares[3])
     slice_grad = jnp.where(me_v.astype(f32) < lengths, slice_grad, 0.0)
     grad_out[...] = slice_grad
     grads_in[me_f] = slice_grad

time: 41.8 us -> 41.8 us (level)
  no operation moved by 1% of the time
where the time goes in v8:
time: 41.8 us; the launch traced here: 41.6 us
  Pallas kernels  38.6 us (92%)
  between operations  1.8 us (4%)
  local copies, waits for them, and re-layouts  1.25 us (3%)
    pallas_call x1, Pallas kernels, body(): pl.pallas_call(functools.partial(kernel, nc, nv, patches), out_shape=[vme...  38.6 us
    unnamed x2, local copies, waits for them, and re-layouts  1.25 us

profile of v8, /device:TPU:1, one launch (start us, length us, event | category | flops | bytes accessed | tf_op | source)
XLA Modules:
  0.0 41.6 jit_solution(1937380413968987475)
XLA Ops:
  0.6 38.6 %shard_map.76 = (f32[1,1]{1,0:T(1,128)S(1)}, f32[32,128]{1,0:T(8,128)S(1)}, f32[200,128]{1,0:T(8,128)S(1)}) custom-call(f32[32,128]{1,0:T(8,128)} %bitcast.19, f32[50,16,128]{2,1,0:T(8,128)} %bitcast.18, s32[8,32]{1,0:T(8,128)} %bitcast.20, s32[8,32]{1,0:T(8,128)} %bitcast.21, s32[1,8]{1,0:T(1,128)} %bitcast.22), custom_call_target="tpu_custom_call" | custom-call | tf_op jit(solution)/shard_map/pallas_call | solution.py:523
  39.2 0.6 %copy.14 = f32[8,1,512]{2,1,0:T(1,128)} copy(f32[8,1,512]{2,1,0:T(1,128)S(1)} %bitcast.17) | data formatting | bytes 32768
  39.9 0.6 %copy.15 = f32[1,4,50,128]{3,1,2,0:T(4,128)} copy(f32[1,4,50,128]{3,1,2,0:T(4,128)S(1)} %bitcast.16) | data formatting | bytes 204800
